TPU v7x, 32 devices: a whole 2x2x4 slice. The times are simulated.
32 devices in a mesh: dp: 8 (over y, x, core), mp: 4 (over z).
Axes of the slice: x: 2, y: 2, z: 4, core: 2. Of those that a mesh axis runs over, the one named last changes fastest.
Arguments:
- patches: bfloat16 [256, 14, 14, 256], P(('dp', 'mp')), may hold values from -6 to 6
- validity: int32 [256, 14, 14], P(('dp', 'mp')), may hold values from 0 to 1, as said below
- norm_gain: bfloat16 [2, 2, 256], P(None, None, 'mp'), may hold values from 0.099609375 to 1.8984375
- norm_shift: bfloat16 [2, 2, 256], P(None, None, 'mp'), may hold values from -3 to 3
- query_key_value_weight: bfloat16 [2, 256, 3, 256], P(None, None, None, 'mp'), may hold values from -0.375 to 0.375
- entry_bias: bfloat16 [2, 2, 256], P(None, None, 'mp'), may hold values from -3 to 3
- stencil: bfloat16 [2, 10, 256], P(None, None, 'mp'), may hold values from -2 to 2
- mixer_weight: bfloat16 [2, 256, 256], P(None, None, 'mp'), may hold values from -1 to 1
- branch_bias: bfloat16 [2, 2, 256], P(None, None, 'mp'), may hold values from -1.75 to 1.75
- expand_weight: bfloat16 [2, 256, 1024], P(None, None, 'mp'), may hold values from -0.375 to 0.375
- hidden_bias: bfloat16 [2, 1024], P(None, 'mp'), may hold values from -3 to 3
- reduce_weight: bfloat16 [2, 1024, 256], P(None, None, 'mp'), may hold values from -0.1875 to 0.1875
- cotangent: bfloat16 [256, 14, 14, 256], P(('dp', 'mp')), may hold values from -6 to 6
Outputs:
- output: bfloat16 [256, 14, 14, 256], P(('dp', 'mp'))
- patch_grad: bfloat16 [256, 14, 14, 256], P(('dp', 'mp'))
- gain_grad: float32 [2, 2, 256], P(None, None, 'mp')
- shift_grad: float32 [2, 2, 256], P(None, None, 'mp')
- packed_grad: float32 [2, 256, 3, 256], P(None, None, None, 'mp')
- entry_grad: float32 [2, 2, 256], P(None, None, 'mp')
- stencil_grad: float32 [2, 10, 256], P(None, None, 'mp')
- mixer_grad: float32 [2, 256, 256], P(None, None, 'mp')
- branch_grad: float32 [2, 2, 256], P(None, None, 'mp')
- expand_grad: float32 [2, 256, 1024], P(None, None, 'mp')
- hidden_grad: float32 [2, 1024], P(None, 'mp')
- reduce_grad: float32 [2, 1024, 256], P(None, None, 'mp')
Inputs may be any that keep to these rules, and one draw needn't show every extreme that they name: validity is 1 on the patches of a crop whose row is below h and whose column is below w, 0 elsewhere, where h and w are whole numbers of 8 to 14 drawn for each crop.
All inputs are finite; a program needn't handle non-finite values.
Results may differ from a plain program's by a relative error of at most 0.025.
Values may be sent and summed in bfloat16 or wider, within the bound.
No kernel may reach another device: no remote copies, remote signals or barrier semaphores. Data moves between devices by JAX's collectives and lax.ppermute only.
A program may use at most 192 MiB of HBM per device.

v0:
```python
import jax
import jax.numpy as jnp
from jax import lax
from jax.sharding import PartitionSpec as P

HEADS = 8
GRID = 14
STRIPE = 7


norm_eps = 1e-05
masked_score = -1e30
root_half = 0.7071067811865476
inverse_root_tau = 0.3989422804014327


def norm_stats(values):
    center = values - jnp.mean(values, axis=-1, keepdims=True)
    spread = jnp.mean(center * center, axis=-1, keepdims=True)
    inverse = lax.rsqrt(spread + norm_eps)
    return (center * inverse, inverse)


def norm_back(grad_normed, normal, inverse, scales):
    scaled = grad_normed * scales
    grad_state = inverse * (
        scaled
        - jnp.mean(scaled, axis=-1, keepdims=True)
        - normal * jnp.mean(scaled * normal, axis=-1, keepdims=True)
    )
    return (
        grad_state,
        jnp.sum(grad_normed * normal, axis=(0, 1, 2)),
        jnp.sum(grad_normed, axis=(0, 1, 2)),
    )


def shifted(values, row_step, col_step):
    extent = values.shape[1]
    padded = jnp.pad(values, ((0, 0), (1, 1), (1, 1), (0, 0)))
    return padded[:, 1 + row_step : 1 + row_step + extent, 1 + col_step : 1 + col_step + extent, :]


def stripe_keep(row_step, col_step, channels):
    row_index = lax.broadcasted_iota(jnp.int32, (GRID, GRID), 0)
    col_index = lax.broadcasted_iota(jnp.int32, (GRID, GRID), 1)
    row_moved = row_index + row_step
    col_moved = col_index + col_step
    inside = (row_moved >= 0) & (row_moved < GRID) & (col_moved >= 0) & (col_moved < GRID)
    across = inside & (row_moved // STRIPE == row_index // STRIPE)
    downward = inside & (col_moved // STRIPE == col_index // STRIPE)
    channel = lax.broadcasted_iota(jnp.int32, (channels,), 0)
    return jnp.where(
        channel[None, None, :] < channels // 2, across[:, :, None], downward[:, :, None]
    ).astype(jnp.float32)


def stencil_apply(valued, taps):
    channels = valued.shape[-1]
    running = jnp.zeros_like(valued) + taps[9]
    for row_step in (-1, 0, 1):
        for col_step in (-1, 0, 1):
            running = running + taps[3 * (row_step + 1) + col_step + 1] * shifted(
                valued, row_step, col_step
            ) * stripe_keep(row_step, col_step, channels)
    return running


def stencil_back(grad_mixed, valued, taps):
    channels = valued.shape[-1]
    tap_grads = []
    value_grad = jnp.zeros_like(valued)
    for row_step in (-1, 0, 1):
        for col_step in (-1, 0, 1):
            keeping = stripe_keep(row_step, col_step, channels)
            tap_grads.append(
                jnp.sum(grad_mixed * shifted(valued, row_step, col_step) * keeping, axis=(0, 1, 2))
            )
            value_grad = value_grad + shifted(
                grad_mixed * keeping * taps[3 * (row_step + 1) + col_step + 1], -row_step, -col_step
            )
    tap_grads.append(jnp.sum(grad_mixed, axis=(0, 1, 2)))
    return (jnp.stack(tap_grads), value_grad)


def gelu(values):
    return 0.5 * values * (1.0 + lax.erf(values * root_half))


def gelu_slope(values):
    return (
        0.5 * (1.0 + lax.erf(values * root_half))
        + values * jnp.exp(-0.5 * values * values) * inverse_root_tau
    )


def split_windows(values):
    crops_here = values.shape[0]
    half = values.shape[3] // 2
    heads = HEADS // 2
    across = values[..., :half].reshape(
        crops_here, GRID // STRIPE, STRIPE * GRID, heads, half // heads
    )
    downward = (
        values[..., half:]
        .reshape(crops_here, GRID, GRID // STRIPE, STRIPE, half)
        .transpose(0, 2, 1, 3, 4)
    )
    downward = downward.reshape(crops_here, GRID // STRIPE, GRID * STRIPE, heads, half // heads)
    return (across, downward)


def join_windows(across, downward):
    crops_here = across.shape[0]
    half = across.shape[3] * across.shape[4]
    upper = across.reshape(crops_here, GRID, GRID, half)
    lower = (
        downward.reshape(crops_here, GRID // STRIPE, GRID, STRIPE, half)
        .transpose(0, 2, 1, 3, 4)
        .reshape(crops_here, GRID, GRID, half)
    )
    return jnp.concatenate([upper, lower], axis=-1)


def key_windows(validity):
    crops_here = validity.shape[0]
    across = validity.reshape(crops_here, GRID // STRIPE, STRIPE * GRID)
    downward = (
        validity.reshape(crops_here, GRID, GRID // STRIPE, STRIPE)
        .transpose(0, 2, 1, 3)
        .reshape(crops_here, GRID // STRIPE, GRID * STRIPE)
    )
    return (across, downward)


def attend(query, keyed, valued, keeping):
    factor = query.shape[-1] ** (-0.5)
    scores = (
        jnp.einsum("cwqhd,cwkhd->cwhqk", query, keyed, preferred_element_type=jnp.float32) * factor
    )
    scores = jnp.where(keeping[:, :, None, None, :] > 0, scores, masked_score)
    peak_score = jnp.max(scores, axis=-1, keepdims=True)
    raised = jnp.exp(scores - peak_score)
    probs = raised / jnp.sum(raised, axis=-1, keepdims=True)
    result = jnp.einsum(
        "cwhqk,cwkhd->cwqhd", probs.astype(jnp.bfloat16), valued, preferred_element_type=jnp.float32
    )
    return (result, probs)


def attend_back(grad_window, query, keyed, valued, probs):
    factor = query.shape[-1] ** (-0.5)
    grad_probs = jnp.einsum(
        "cwqhd,cwkhd->cwhqk", grad_window, valued, preferred_element_type=jnp.float32
    )
    grad_value = jnp.einsum(
        "cwhqk,cwqhd->cwkhd",
        probs.astype(jnp.bfloat16),
        grad_window,
        preferred_element_type=jnp.float32,
    )
    grad_scores = (
        probs * (grad_probs - jnp.sum(grad_probs * probs, axis=-1, keepdims=True))
    ).astype(jnp.bfloat16)
    grad_query = (
        jnp.einsum("cwhqk,cwkhd->cwqhd", grad_scores, keyed, preferred_element_type=jnp.float32)
        * factor
    )
    grad_key = (
        jnp.einsum("cwhqk,cwqhd->cwkhd", grad_scores, query, preferred_element_type=jnp.float32)
        * factor
    )
    return (grad_query, grad_key, grad_value)


def forward_layer(state, keep_pair, weights):
    (
        scales,
        offsets,
        combined_projection_complete,
        entry_full,
        stencil_full,
        mixer_full,
        branch_full,
        expand_full,
        hidden_full,
        reduce_full,
    ) = weights
    scales = scales.astype(jnp.float32)
    offsets = offsets.astype(jnp.float32)
    normal_one, inverse_one = norm_stats(state)
    normalized_input_reduced = (normal_one * scales[0] + offsets[0]).astype(jnp.bfloat16)
    combined_projection = jnp.einsum(
        "zaht,typ->zahyp",
        normalized_input_reduced,
        combined_projection_complete,
        preferred_element_type=jnp.float32,
    )
    entry = entry_full.astype(jnp.float32)
    query_low = (combined_projection[..., 0, :] + entry[0]).astype(jnp.bfloat16)
    key_low = combined_projection[..., 1, :].astype(jnp.bfloat16)
    value_low = (combined_projection[..., 2, :] + entry[1]).astype(jnp.bfloat16)
    query_across, query_down = split_windows(query_low)
    key_across, key_down = split_windows(key_low)
    value_across, value_down = split_windows(value_low)
    result_across, probs_across = attend(query_across, key_across, value_across, keep_pair[0])
    result_down, probs_down = attend(query_down, key_down, value_down, keep_pair[1])
    taps = stencil_full.astype(jnp.float32)
    mixed_low = (
        join_windows(result_across, result_down)
        + stencil_apply(value_low.astype(jnp.float32), taps)
    ).astype(jnp.bfloat16)
    branch = branch_full.astype(jnp.float32)
    middle = state + (
        jnp.einsum("cijd,dk->cijk", mixed_low, mixer_full, preferred_element_type=jnp.float32)
        + branch[0]
    )
    normal_two, inverse_two = norm_stats(middle)
    normed_two = (normal_two * scales[1] + offsets[1]).astype(jnp.bfloat16)
    inner = jnp.einsum(
        "cijd,df->cijf", normed_two, expand_full, preferred_element_type=jnp.float32
    ) + hidden_full.astype(jnp.float32)
    hidden_low = gelu(inner).astype(jnp.bfloat16)
    result = middle + (
        jnp.einsum("cijf,fd->cijd", hidden_low, reduce_full, preferred_element_type=jnp.float32)
        + branch[1]
    )
    saved = (
        normal_one,
        inverse_one,
        normalized_input_reduced,
        query_low,
        key_low,
        value_low,
        probs_across,
        probs_down,
        mixed_low,
        normal_two,
        inverse_two,
        normed_two,
        inner,
        hidden_low,
    )
    return (result, saved)


def backward_layer(grad_out, saved, weights):
    (
        scales,
        offsets,
        combined_projection_complete,
        entry_full,
        stencil_full,
        mixer_full,
        branch_full,
        expand_full,
        hidden_full,
        reduce_full,
    ) = weights
    (
        normal_one,
        inverse_one,
        normalized_input_reduced,
        query_low,
        key_low,
        value_low,
        probs_across,
        probs_down,
        mixed_low,
        normal_two,
        inverse_two,
        normed_two,
        inner,
        hidden_low,
    ) = saved
    scales = scales.astype(jnp.float32)
    grad_second = grad_out.astype(jnp.bfloat16)
    reduce_part = jnp.einsum(
        "cijf,cijd->fd", hidden_low, grad_second, preferred_element_type=jnp.float32
    )
    bias_second = jnp.sum(grad_second.astype(jnp.float32), axis=(0, 1, 2))
    grad_hidden = jnp.einsum(
        "cijd,fd->cijf", grad_second, reduce_full, preferred_element_type=jnp.float32
    )
    grad_inner = (grad_hidden * gelu_slope(inner)).astype(jnp.bfloat16)
    expand_part = jnp.einsum(
        "cijd,cijf->df", normed_two, grad_inner, preferred_element_type=jnp.float32
    )
    hidden_part = jnp.sum(grad_inner.astype(jnp.float32), axis=(0, 1, 2))
    grad_normed_two = jnp.einsum(
        "cijf,df->cijd", grad_inner, expand_full, preferred_element_type=jnp.float32
    )
    grad_state_two, gain_two, offset_two = norm_back(
        grad_normed_two, normal_two, inverse_two, scales[1]
    )
    grad_middle = grad_out + grad_state_two
    grad_first = grad_middle.astype(jnp.bfloat16)
    mixer_part = jnp.einsum(
        "cijd,cijk->dk", mixed_low, grad_first, preferred_element_type=jnp.float32
    )
    bias_first = jnp.sum(grad_first.astype(jnp.float32), axis=(0, 1, 2))
    grad_mixed = jnp.einsum(
        "cijk,dk->cijd", grad_first, mixer_full, preferred_element_type=jnp.float32
    ).astype(jnp.bfloat16)
    stencil_part, value_from_stencil = stencil_back(
        grad_mixed.astype(jnp.float32),
        value_low.astype(jnp.float32),
        stencil_full.astype(jnp.float32),
    )
    grad_across, grad_down = split_windows(grad_mixed)
    query_across, query_down = split_windows(query_low)
    key_across, key_down = split_windows(key_low)
    value_across, value_down = split_windows(value_low)
    dq_across, dk_across, dv_across = attend_back(
        grad_across, query_across, key_across, value_across, probs_across
    )
    dq_down, dk_down, dv_down = attend_back(grad_down, query_down, key_down, value_down, probs_down)
    grad_query = join_windows(dq_across, dq_down).astype(jnp.bfloat16)
    grad_key = join_windows(dk_across, dk_down).astype(jnp.bfloat16)
    grad_value = (join_windows(dv_across, dv_down) + value_from_stencil).astype(jnp.bfloat16)
    gradient_combined_projection = jnp.stack([grad_query, grad_key, grad_value], axis=3)
    packed_part = jnp.einsum(
        "rtlo,rtlvx->ovx",
        normalized_input_reduced,
        gradient_combined_projection,
        preferred_element_type=jnp.float32,
    )
    entry_part = jnp.stack(
        [
            jnp.sum(grad_query.astype(jnp.float32), axis=(0, 1, 2)),
            jnp.sum(grad_value.astype(jnp.float32), axis=(0, 1, 2)),
        ]
    )
    grad_normed = jnp.einsum(
        "xthzy,nzy->xthn",
        gradient_combined_projection,
        combined_projection_complete,
        preferred_element_type=jnp.float32,
    )
    grad_state_one, gain_one, offset_one = norm_back(
        grad_normed, normal_one, inverse_one, scales[0]
    )
    grad_input = grad_middle + grad_state_one
    layer_grads = (
        jnp.stack([gain_one, gain_two]),
        jnp.stack([offset_one, offset_two]),
        packed_part,
        entry_part,
        stencil_part,
        mixer_part,
        jnp.stack([bias_first, bias_second]),
        expand_part,
        hidden_part,
        reduce_part,
    )
    return (grad_input, layer_grads)


def take_share(summed, axis_dim):
    share = summed.shape[axis_dim] // lax.axis_size("mp")
    return lax.dynamic_slice_in_dim(summed, lax.axis_index("mp") * share, share, axis_dim)


def body(
    patches,
    validity,
    norm_gain,
    norm_shift,
    query_key_value_weight,
    entry_bias,
    stencil,
    mixer_weight,
    branch_bias,
    expand_weight,
    hidden_bias,
    reduce_weight,
    cotangent,
):
    keep_pair = key_windows(validity)
    layer_count = query_key_value_weight.shape[0]
    state = patches.astype(jnp.float32)
    fetched = []
    kept_layers = []
    for layer in range(layer_count):
        weights = (
            lax.all_gather(norm_gain[layer], "mp", axis=1, tiled=True),
            lax.all_gather(norm_shift[layer], "mp", axis=1, tiled=True),
            lax.all_gather(query_key_value_weight[layer], "mp", axis=2, tiled=True),
            lax.all_gather(entry_bias[layer], "mp", axis=1, tiled=True),
            lax.all_gather(stencil[layer], "mp", axis=1, tiled=True),
            lax.all_gather(mixer_weight[layer], "mp", axis=1, tiled=True),
            lax.all_gather(branch_bias[layer], "mp", axis=1, tiled=True),
            lax.all_gather(expand_weight[layer], "mp", axis=1, tiled=True),
            lax.all_gather(hidden_bias[layer], "mp", axis=0, tiled=True),
            lax.all_gather(reduce_weight[layer], "mp", axis=1, tiled=True),
        )
        fetched.append(weights)
        state, saved = forward_layer(state, keep_pair, weights)
        kept_layers.append(saved)
    output = state.astype(jnp.bfloat16)
    gradient = cotangent.astype(jnp.float32)
    all_grads = [None] * layer_count
    for layer in reversed(range(layer_count)):
        weights = fetched[layer]
        gradient, layer_grads = backward_layer(gradient, kept_layers[layer], weights)
        all_grads[layer] = layer_grads
    stacked = [
        jnp.stack([member_grads[member] for member_grads in all_grads]) for member in range(10)
    ]
    share_dims = (2, 2, 3, 2, 2, 2, 2, 2, 1, 2)
    summed = lax.psum(
        (
            stacked[0],
            stacked[1],
            stacked[2],
            stacked[3],
            stacked[4],
            stacked[5],
            stacked[6],
            stacked[7],
            stacked[8],
            stacked[9],
        ),
        ("dp", "mp"),
    )
    weight_sums = tuple(
        (take_share(member, axis_dim) for member, axis_dim in zip(summed, share_dims))
    )
    return (output, gradient.astype(jnp.bfloat16)) + tuple(weight_sums)


def solution(mesh):
    placed = (
        P(("dp", "mp"), None, None, None),
        P(("dp", "mp"), None, None),
        P(None, None, "mp"),
        P(None, None, "mp"),
        P(None, None, None, "mp"),
        P(None, None, "mp"),
        P(None, None, "mp"),
        P(None, None, "mp"),
        P(None, None, "mp"),
        P(None, None, "mp"),
        P(None, "mp"),
        P(None, None, "mp"),
        P(("dp", "mp"), None, None, None),
    )
    return jax.shard_map(
        body,
        mesh=mesh,
        in_specs=placed,
        out_specs=(
            P(("dp", "mp"), None, None, None),
            P(("dp", "mp"), None, None, None),
            P(None, None, "mp"),
            P(None, None, "mp"),
            P(None, None, None, "mp"),
            P(None, None, "mp"),
            P(None, None, "mp"),
            P(None, None, "mp"),
            P(None, None, "mp"),
            P(None, None, "mp"),
            P(None, "mp"),
            P(None, None, "mp"),
        ),
        check_vma=False,
    )
```

profile of v0, /device:TPU:0, one launch (start us, length us, event | category | flops | bytes accessed | tf_op | source)
XLA Modules:
  0.0 944.0 jit_solution(16267231311566018731)
XLA Ops:
  15.7 12.6 %all-gather.18 = bf16[1,1024]{1,0:T(2,128)(2,1)S(1)} all-gather(bf16[1,256]{1,0:T(2,128)(2,1)S(1)} %get-tuple-element.240), channel_id=20, replica_groups=mesh['dp'=8,'mp'=4] {'mp'}, dimensions={1}, use_global_device_ids=true | all-gather | bytes 2560 | tf_op jit(solution)/shard_map/all_gather | solution.py:394
  28.9 7.6 all-gather.8
  44.0 14.1 %all-gather.15 = bf16[1,256,256]{1,2,0:T(8,128)(2,1)} all-gather(bf16[1,256,64]{1,2,0:T(8,128)(2,1)S(1)} %get-tuple-element.213), channel_id=17, replica_groups=mesh['dp'=8,'mp'=4] {'mp'}, dimensions={2}, use_global_device_ids=true | all-gather | bytes 163840 | tf_op jit(solution)/shard_map/all_gather | solution.py:391
  58.1 13.6 %all-gather = bf16[1,2,256]{1,0,2:T(2,128)(2,1)S(1)} all-gather(bf16[1,2,64]{1,0,2:T(2,128)(2,1)S(1)} %copy.627), channel_id=2, replica_groups=mesh['dp'=8,'mp'=4] {'mp'}, dimensions={2}, use_global_device_ids=true | all-gather | bytes 1280 | tf_op jit(solution)/shard_map/all_gather | solution.py:386
  76.0 13.3 %all-gather.1 = bf16[1,2,256]{1,0,2:T(2,128)(2,1)S(1)} all-gather(bf16[1,2,64]{1,0,2:T(2,128)(2,1)S(1)} %copy.628), channel_id=3, replica_groups=mesh['dp'=8,'mp'=4] {'mp'}, dimensions={2}, use_global_device_ids=true | all-gather | bytes 1280 | tf_op jit(solution)/shard_map/all_gather | solution.py:387
  93.7 13.5 %all-gather.3 = bf16[1,2,256]{1,0,2:T(2,128)(2,1)S(1)} all-gather(bf16[1,2,64]{1,0,2:T(2,128)(2,1)S(1)} %copy.629), channel_id=5, replica_groups=mesh['dp'=8,'mp'=4] {'mp'}, dimensions={2}, use_global_device_ids=true | all-gather | bytes 1280 | tf_op jit(solution)/shard_map/all_gather | solution.py:389
  110.9 13.4 %all-gather.6 = bf16[1,2,256]{1,0,2:T(2,128)(2,1)S(1)} all-gather(bf16[1,2,64]{1,0,2:T(2,128)(2,1)S(1)} %copy.631), channel_id=8, replica_groups=mesh['dp'=8,'mp'=4] {'mp'}, dimensions={2}, use_global_device_ids=true | all-gather | bytes 1280 | tf_op jit(solution)/shard_map/all_gather | solution.py:392
  127.6 13.5 %all-gather.4 = bf16[1,10,256]{1,0,2:T(2,128)(2,1)S(1)} all-gather(bf16[1,10,64]{1,0,2:T(2,128)(2,1)S(1)} %copy.630), channel_id=6, replica_groups=mesh['dp'=8,'mp'=4] {'mp'}, dimensions={2}, use_global_device_ids=true | all-gather | bytes 6400 | tf_op jit(solution)/shard_map/all_gather | solution.py:390
  141.3 10.2 %slice_reduce_fusion.31 = (f32[256]{0:T(256)}, f32[256]{0:T(256)}, f32[256]{0:T(256)}, f32[256]{0:T(256)}, f32[256]{0:T(256)}, /*index=5*/f32[256]{0:T(256)}, f3...) fusion(f32[1,10,256]{1,0,2:T(1,128)S(1)} %convert_element_type.534), kind=kLoop, calls=%fused_computation.407 | loop fusion | bytes 20480 | tf_op jit(solution)/shard_map/slice | solution.py:60
  151.5 13.3 %all-gather.10 = bf16[1,2,256]{1,0,2:T(2,128)(2,1)S(1)} all-gather(bf16[1,2,64]{1,0,2:T(2,128)(2,1)S(1)} %copy.632), channel_id=12, replica_groups=mesh['dp'=8,'mp'=4] {'mp'}, dimensions={2}, use_global_device_ids=true | all-gather | bytes 1280 | tf_op jit(solution)/shard_map/all_gather | solution.py:386
  168.2 13.3 %all-gather.11 = bf16[1,2,256]{1,0,2:T(2,128)(2,1)S(1)} all-gather(bf16[1,2,64]{1,0,2:T(2,128)(2,1)S(1)} %copy.633), channel_id=13, replica_groups=mesh['dp'=8,'mp'=4] {'mp'}, dimensions={2}, use_global_device_ids=true | all-gather | bytes 1280 | tf_op jit(solution)/shard_map/all_gather | solution.py:387
  184.9 13.9 %all-gather.13 = bf16[1,2,256]{1,0,2:T(2,128)(2,1)S(1)} all-gather(bf16[1,2,64]{1,0,2:T(2,128)(2,1)S(1)} %copy.635), channel_id=15, replica_groups=mesh['dp'=8,'mp'=4] {'mp'}, dimensions={2}, use_global_device_ids=true | all-gather | bytes 1280 | tf_op jit(solution)/shard_map/all_gather | solution.py:389
  203.1 13.3 %all-gather.16 = bf16[1,2,256]{1,0,2:T(2,128)(2,1)S(1)} all-gather(bf16[1,2,64]{1,0,2:T(2,128)(2,1)S(1)} %copy.637), channel_id=18, replica_groups=mesh['dp'=8,'mp'=4] {'mp'}, dimensions={2}, use_global_device_ids=true | all-gather | bytes 1280 | tf_op jit(solution)/shard_map/all_gather | solution.py:392
  219.7 13.9 %all-gather.14 = bf16[1,10,256]{1,0,2:T(2,128)(2,1)S(1)} all-gather(bf16[1,10,64]{1,0,2:T(2,128)(2,1)S(1)} %copy.636), channel_id=16, replica_groups=mesh['dp'=8,'mp'=4] {'mp'}, dimensions={2}, use_global_device_ids=true | all-gather | bytes 6400 | tf_op jit(solution)/shard_map/all_gather | solution.py:390
  233.7 10.2 %slice_reduce_fusion.13 = (f32[256]{0:T(256)}, f32[256]{0:T(256)}, f32[256]{0:T(256)}, f32[256]{0:T(256)}, f32[256]{0:T(256)}, /*index=5*/f32[256]{0:T(256)}, f3...) fusion(f32[1,10,256]{1,0,2:T(1,128)S(1)} %convert_element_type.540), kind=kLoop, calls=%fused_computation.389 | loop fusion | bytes 20480 | tf_op jit(solution)/shard_map/slice | solution.py:60
  244.0 14.5 %all-gather.5 = bf16[1,256,256]{1,2,0:T(8,128)(2,1)} all-gather(bf16[1,256,64]{1,2,0:T(8,128)(2,1)S(1)} %get-tuple-element.214), channel_id=7, replica_groups=mesh['dp'=8,'mp'=4] {'mp'}, dimensions={2}, use_global_device_ids=true | all-gather | bytes 163840 | tf_op jit(solution)/shard_map/all_gather | solution.py:391
  258.6 15.9 %all-gather.12 = bf16[1,256,3,256]{1,3,2,0:T(8,128)(2,1)} all-gather(bf16[1,256,3,64]{1,3,2,0:T(8,128)(2,1)S(1)} %get-tuple-element.211), channel_id=14, replica_groups=mesh['dp'=8,'mp'=4] {'mp'}, dimensions={3}, use_global_device_ids=true | all-gather | bytes 491520 | tf_op jit(solution)/shard_map/all_gather | solution.py:388
  274.5 15.9 %all-gather.19 = bf16[1,1024,256]{1,2,0:T(8,128)(2,1)} all-gather(bf16[1,1024,64]{1,2,0:T(8,128)(2,1)S(1)} %get-tuple-element.207), channel_id=21, replica_groups=mesh['dp'=8,'mp'=4] {'mp'}, dimensions={2}, use_global_device_ids=true | all-gather | bytes 655360 | tf_op jit(solution)/shard_map/all_gather | solution.py:395
  290.4 16.6 %all-gather.17 = bf16[1,256,1024]{2,1,0:T(8,128)(2,1)} all-gather(bf16[1,256,256]{2,1,0:T(8,128)(2,1)S(1)} %get-tuple-element.209), channel_id=19, replica_groups=mesh['dp'=8,'mp'=4] {'mp'}, dimensions={2}, use_global_device_ids=true | all-gather | bytes 655360 | tf_op jit(solution)/shard_map/all_gather | solution.py:393
  307.0 14.3 %all-gather.2 = bf16[1,256,3,256]{1,3,2,0:T(8,128)(2,1)S(1)} all-gather(bf16[1,256,3,64]{1,3,2,0:T(8,128)(2,1)S(1)} %get-tuple-element.212), channel_id=4, replica_groups=mesh['dp'=8,'mp'=4] {'mp'}, dimensions={3}, use_global_device_ids=true | all-gather | bytes 491520 | tf_op jit(solution)/shard_map/all_gather | solution.py:388
  321.3 15.5 %all-gather.9 = bf16[1,1024,256]{1,2,0:T(8,128)(2,1)} all-gather(bf16[1,1024,64]{1,2,0:T(8,128)(2,1)S(1)} %get-tuple-element.208), channel_id=11, replica_groups=mesh['dp'=8,'mp'=4] {'mp'}, dimensions={2}, use_global_device_ids=true | all-gather | bytes 655360 | tf_op jit(solution)/shard_map/all_gather | solution.py:395
  336.9 15.7 %all-gather.7 = bf16[1,256,1024]{2,1,0:T(8,128)(2,1)} all-gather(bf16[1,256,256]{2,1,0:T(8,128)(2,1)S(1)} %get-tuple-element.210), channel_id=9, replica_groups=mesh['dp'=8,'mp'=4] {'mp'}, dimensions={2}, use_global_device_ids=true | all-gather | bytes 655360 | tf_op jit(solution)/shard_map/all_gather | solution.py:393
  409.4 4.8 fusion.263
  516.9 9.1 fusion.122
  531.8 5.0 convert_reduce_fusion.2
  545.6 7.0 fusion.59
  636.1 7.1 convert_reduce_fusion.9
  666.8 7.3 fusion.86
  755.0 7.1 convert_reduce_fusion.10
  772.9 9.3 convert_reduce_fusion.1
  813.9 40.4 %all-reduce.18 = (f32[2,2,256]{2,1,0:T(2,128)S(1)}, f32[2,2,256]{2,1,0:T(2,128)S(1)}, f32[2,2,256]{2,1,0:T(2,128)S(1)}, f32[2,10,256]{2,1,0:T(8,128)S(1)}, f32[2...) all-reduce(f32[2,2,256]{2,1,0:T(2,128)S(1)} %pad_maximum_fusion.8, ...), channel_id=1, replica_groups=mesh['dp'=8,'mp'=4] {'dp','mp'}, use_global_device_ids=true, to_apply=%region_32.33 | all-reduce | flops 11264 | bytes 90112 | tf_op jit(solution)/shard_map/psum | solution.py:411
  858.1 71.2 %all-reduce.22.cloned.1.call-done = (f32[2,256,3,256]{3,1,2,0:T(8,128)}, f32[2,256,256]{2,1,0:T(8,128)}, f32[2,256,1024]{2,1,0:T(8,128)}, f32[2,1024,256]{2,1,0:T(8,128)}) async-done(((f32[2,256,3,256]{3,1,2,0:T(8,128)}, f32[2,256,256]{2,1,0:T(8,128)}, f32[2,256,1024]{2,1,0:T(8,128)}, f32[2,1024,256]{2,1,0:T(8,128)}), (f32[2,256,3,256]{3,1,2,0:T(8,128)}, f32[2,256,256]{2,1,0:T(8,128)}, ...) | async-done | bytes 6291472 | tf_op jit(solution)/shard_map/psum | solution.py:411
  (758 shorter events, 460.4 us)
Async XLA Ops:
  7.2 36.1 %copy-start = (bf16[8,14,14,256]{3,0,2,1:T(8,128)(2,1)S(1)}, bf16[8,14,14,256]{3,0,2,1:T(8,128)(2,1)}, u32[]{:S(2)}) copy-start(bf16[8,14,14,256]{3,0,2,1:T(8,128)(2,1)} %param.13) | copy-start | bytes 2408452
  7.2 36.8 %copy-start.132 = (bf16[2,256,64]{1,2,0:T(8,128)(2,1)S(1)}, bf16[2,256,64]{1,2,0:T(8,128)(2,1)}, u32[]{:S(2)}) copy-start(bf16[2,256,64]{1,2,0:T(8,128)(2,1)} %param.20) | copy-start | bytes 196612
  7.2 922.2 %all-reduce.22.cloned.1.call-start = ((), (), s32[]{:S(2)}) async-start(), calls=%async_computation | async-start | bytes 12582912 | tf_op jit(solution)/shard_map/psum | solution.py:411
  43.3 309.2 %copy-start.76 = (f32[8,14,14]{2,1,0:T(8,128)}, f32[8,14,14]{2,1,0:T(8,128)S(1)}, u32[]{:S(2)}) copy-start(f32[8,14,14]{2,1,0:T(8,128)S(1)} %broadcast_multiply_fusion.11) | copy-start | bytes 18820
  44.0 308.5 %copy-start.92 = (f32[8,14,14]{2,1,0:T(8,128)}, f32[8,14,14]{2,1,0:T(8,128)S(1)}, u32[]{:S(2)}) copy-start(f32[8,14,14]{2,1,0:T(8,128)S(1)} %add_rsqrt_fusion.3) | copy-start | bytes 18820
  76.0 276.5 %copy-start.139 = (f32[256]{0:T(256)}, f32[256]{0:T(256)S(1)}, u32[]{:S(2)}) copy-start(f32[256]{0:T(256)S(1)} %get-tuple-element.133) | copy-start | bytes 3076
  93.7 258.9 %copy-start.170 = (f32[256]{0:T(256)}, f32[256]{0:T(256)S(1)}, u32[]{:S(2)}) copy-start(f32[256]{0:T(256)S(1)} %get-tuple-element.135) | copy-start | bytes 3076
  181.7 76.9 %copy-start.131 = (bf16[2,256,3,64]{1,3,2,0:T(8,128)(2,1)S(1)}, bf16[2,256,3,64]{1,3,2,0:T(8,128)(2,1)}, u32[]{:S(2)}) copy-start(bf16[2,256,3,64]{1,3,2,0:T(8,128)(2,1)} %param.17) | copy-start | bytes 589828
  184.9 73.6 %copy-start.127 = (bf16[2,256,256]{2,1,0:T(8,128)(2,1)S(1)}, bf16[2,256,256]{2,1,0:T(8,128)(2,1)}, u32[]{:S(2)}) copy-start(bf16[2,256,256]{2,1,0:T(8,128)(2,1)} %param.22) | copy-start | bytes 786436
  198.9 59.7 %copy-start.128 = (bf16[2,1024,64]{1,2,0:T(8,128)(2,1)S(1)}, bf16[2,1024,64]{1,2,0:T(8,128)(2,1)}, u32[]{:S(2)}) copy-start(bf16[2,1024,64]{1,2,0:T(8,128)(2,1)} %param.24) | copy-start | bytes 786436
  321.3 32.4 %copy-start.85 = (bf16[1,256,3,256]{1,3,2,0:T(8,128)(2,1)}, bf16[1,256,3,256]{1,3,2,0:T(8,128)(2,1)S(1)}, u32[]{:S(2)}) copy-start(bf16[1,256,3,256]{1,3,2,0:T(8,128)(2,1)S(1)} %all-gather.2) | copy-start | bytes 1179652
  355.5 71.1 %copy-start.8 = (f32[8,14,14,256]{3,2,1,0:T(8,128)}, f32[8,14,14,256]{3,2,1,0:T(8,128)S(1)}, u32[]{:S(2)}) copy-start(f32[8,14,14,256]{3,2,1,0:T(8,128)S(1)} %get-tuple-element.170) | copy-start | bytes 4816900
  379.0 13.9 %copy-start.58 = (bf16[8,2,98,4,32]{2,4,3,1,0:T(8,128)(2,1)}, bf16[8,2,98,4,32]{2,4,3,1,0:T(8,128)(2,1)S(1)}, u32[]{:S(2)}) copy-start(bf16[8,2,98,4,32]{2,4,3,1,0:T(8,128)(2,1)S(1)} %copy.425) | copy-start | bytes 1204228
  426.0 210.1 %copy-start.122 = (f32[14,14]{1,0:T(8,128)}, f32[14,14]{1,0:T(8,128)S(1)}, u32[]{:S(2)}) copy-start(f32[14,14]{1,0:T(8,128)S(1)} %get-tuple-element.250) | copy-start | bytes 2356
  426.6 240.0 %copy-start.14 = (f32[14,14,256]{2,1,0:T(8,128)}, f32[14,14,256]{2,1,0:T(8,128)S(1)}, u32[]{:S(2)}) copy-start(f32[14,14,256]{2,1,0:T(8,128)S(1)} %get-tuple-element.251) | copy-start | bytes 602116
  426.6 240.0 %copy-start.16 = (f32[14,14,256]{2,1,0:T(8,128)}, f32[14,14,256]{2,1,0:T(8,128)S(1)}, u32[]{:S(2)}) copy-start(f32[14,14,256]{2,1,0:T(8,128)S(1)} %get-tuple-element.252) | copy-start | bytes 602116
  426.6 240.0 %copy-start.18 = (f32[14,14,256]{2,1,0:T(8,128)}, f32[14,14,256]{2,1,0:T(8,128)S(1)}, u32[]{:S(2)}) copy-start(f32[14,14,256]{2,1,0:T(8,128)S(1)} %get-tuple-element.253) | copy-start | bytes 602116
  516.9 9.1 copy-start.89
  516.9 9.1 copy-start.204
  526.5 15.1 %copy-start.4 = (f32[8,14,14,256]{3,2,1,0:T(8,128)}, f32[8,14,14,256]{3,2,1,0:T(8,128)S(1)}, u32[]{:S(2)}) copy-start(f32[8,14,14,256]{3,2,1,0:T(8,128)S(1)} %get-tuple-element.274) | copy-start | bytes 4816900
  552.6 83.5 %copy-start.10 = (bf16[8,14,14,256]{3,2,1,0:T(8,128)(2,1)}, bf16[8,14,14,256]{3,2,1,0:T(8,128)(2,1)S(1)}, u32[]{:S(2)}) copy-start(bf16[8,14,14,256]{3,2,1,0:T(8,128)(2,1)S(1)} %get-tuple-element.278) | copy-start | bytes 2408452
  674.1 80.8 %copy-start.12 = (bf16[8,14,14,256]{3,2,1,0:T(8,128)(2,1)}, bf16[8,14,14,256]{3,2,1,0:T(8,128)(2,1)S(1)}, u32[]{:S(2)}) copy-start(bf16[8,14,14,256]{3,2,1,0:T(8,128)(2,1)S(1)} %get-tuple-element.284) | copy-start | bytes 2408452
  704.3 45.5 %copy-start.42 = (bf16[8,2,98,4,32]{2,4,3,1,0:T(8,128)(2,1)}, bf16[8,2,98,4,32]{2,4,3,1,0:T(8,128)(2,1)S(1)}, u32[]{:S(2)}) copy-start(bf16[8,2,98,4,32]{2,4,3,1,0:T(8,128)(2,1)S(1)} %fusion.149) | copy-start | bytes 1204228
  772.9 9.3 copy-start.55
  772.9 9.3 copy-start.86
  772.9 10.2 %copy-start.232 = (bf16[8,14,14,1024]{3,2,1,0:T(8,128)(2,1)S(1)}, bf16[8,14,14,1024]{3,2,1,0:T(8,128)(2,1)}, u32[]{:S(2)}) copy-start(bf16[8,14,14,1024]{3,2,1,0:T(8,128)(2,1)} %get-tuple-element.275) | copy-start | bytes 9633796
  803.3 9.0 copy-start.184
  803.3 9.0 copy-start.185
  803.3 9.1 copy-start.183
  803.3 10.4 %copy-start.186 = (f32[256]{0:T(256)S(1)}, f32[256]{0:T(256)}, u32[]{:S(2)}) copy-start(f32[256]{0:T(256)} %get-tuple-element.164) | copy-start | bytes 3076
  803.3 10.5 %copy-start.202 = (f32[1024]{0:T(1024)S(1)}, f32[1024]{0:T(1024)}, u32[]{:S(2)}) copy-start(f32[1024]{0:T(1024)} %get-tuple-element.289) | copy-start | bytes 12292
  803.3 10.5 %copy-start.203 = (f32[1024]{0:T(1024)S(1)}, f32[1024]{0:T(1024)}, u32[]{:S(2)}) copy-start(f32[1024]{0:T(1024)} %get-tuple-element.291) | copy-start | bytes 12292
  (204 other events, 659.9 us)
Sparse Core Ops, SparseCore 0:
  771.9 157.4 all-reduce.21
where the time goes:
time: 955 us; the launch traced here: 944 us
  local copies, waits for them, and re-layouts  328 us (34%)
  blocking collectives  318 us (33%)
  matrix products  128 us (13%)
  other arithmetic  81.6 us (9%)
  waiting for transfers between devices  71.2 us (7%)
  between operations  17 us (2%)
    psum x1, waiting for transfers between devices, body(): lax.psum((stacked[0], stacked[1], stacked[2], stacked[3], stacked[4], sta...  71.2 us
    reshape x16, local copies, waits for them, and re-layouts, split_windows(): downward.reshape(crops_here, GRID // STRIPE, GRID * STRIPE, heads, half /...  48.8 us
    reshape x16, local copies, waits for them, and re-layouts, split_windows(): values[..., :half]  44 us
    psum x1, blocking collectives, body(): lax.psum((stacked[0], stacked[1], stacked[2], stacked[3], stacked[4], sta...  40.4 us
    reshape x10, local copies, waits for them, and re-layouts, join_windows(): upper = across.reshape(crops_here, GRID, GRID, half)  35.7 us
    all_gather x2, blocking collectives, body(): lax.all_gather(expand_weight[layer], 'mp', axis=1, tiled=True)  32.2 us
    all_gather x2, blocking collectives, body(): lax.all_gather(reduce_weight[layer], 'mp', axis=1, tiled=True)  31.4 us
    all_gather x2, blocking collectives, body(): lax.all_gather(query_key_value_weight[layer], 'mp', axis=2, tiled=True)  30.2 us
  transfers between devices with their start and end apart: 1, of which 1 were waited for; matrix products, arithmetic and copies ran while one was open for 5% of the time, Pallas kernels for 0%

commit v1 on v0

v1 whole, which is shorter than its diff:
```python
import functools

import jax
import jax.numpy as jnp
from jax import lax
from jax.experimental import pallas as pl
from jax.experimental.pallas import tpu as pltpu
from jax.sharding import PartitionSpec as P

GRID = 14
STRIPE = 7
MINOR = 16
TOK = GRID * MINOR
WIN = STRIPE * MINOR
HALF_HEADS = 4
HEAD = 32
D = 256
FF = 1024
CB = 2

norm_eps = 1e-05
masked_score = -1e30
root_half = 0.7071067811865476
inverse_root_tau = 0.3989422804014327
log2_e = 1.4426950408889634
factor = HEAD**-0.5

f32 = jnp.float32
bf16 = jnp.bfloat16

ATTN_ROWS = 288
FF_ROWS = 512
GRAD_ATTN_ROWS = 320
GAIN, SHIFT, ENTRY, TAPS, BRANCH, HIDDEN = 0, 2, 4, 6, 16, 18


def dot(a, b):
    return lax.dot_general(a, b, (((1,), (0,)), ((), ())), preferred_element_type=f32)


def dot_nt(a, b):
    return lax.dot_general(a, b, (((1,), (1,)), ((), ())), preferred_element_type=f32)


def dot_tn(a, b):
    return lax.dot_general(a, b, (((0,), (0,)), ((), ())), preferred_element_type=f32)


def norm(x):
    center = x - jnp.mean(x, axis=-1, keepdims=True)
    spread = jnp.mean(center * center, axis=-1, keepdims=True)
    inverse = lax.rsqrt(spread + norm_eps)
    return center * inverse, inverse


def norm_back(grad, normal, inverse, gain):
    scaled = grad * gain
    return inverse * (
        scaled
        - jnp.mean(scaled, axis=-1, keepdims=True)
        - normal * jnp.mean(scaled * normal, axis=-1, keepdims=True)
    )


def column_sum(x):
    return jnp.sum(x, axis=0, keepdims=True)


def grid_transpose():
    row = lax.broadcasted_iota(jnp.int32, (TOK, TOK), 0)
    col = lax.broadcasted_iota(jnp.int32, (TOK, TOK), 1)
    hit = (row // MINOR == col % MINOR) & (row % MINOR == col // MINOR)
    return hit.astype(f32).astype(bf16)


def minor_inside(rows, lanes):
    cell = lax.broadcasted_iota(jnp.int32, (rows, lanes), 0) % MINOR
    return cell < GRID


def key_bias(major_end, minor_end, window):
    row = lax.broadcasted_iota(jnp.int32, (WIN, 128), 0)
    major = row // MINOR + window * STRIPE
    minor = row % MINOR
    return jnp.where((major < major_end) & (minor < minor_end), 0.0, masked_score)


def heads_apart(x):
    lane = lax.broadcasted_iota(jnp.int32, (WIN, 128), 1) // HEAD
    wide = x.astype(f32)
    rest = jnp.zeros((128 - WIN, 128), bf16)
    blocks = []
    for head in range(HALF_HEADS):
        blocks.append(jnp.where(lane == head, wide, 0.0).astype(bf16))
        blocks.append(rest)
    return jnp.concatenate(blocks, axis=0)


def by_head(flat, probs):
    turned = flat.astype(f32).T.astype(bf16)
    parts = []
    for head in range(HALF_HEADS):
        parts.append(
            dot(turned[head * HEAD : (head + 1) * HEAD], probs[:, head * 128 : (head + 1) * 128])
        )
    return jnp.concatenate(parts, axis=0).T[:WIN]


def attend(query, key, value, bias):
    scores = dot_nt(key, heads_apart(query)) * (factor * log2_e)
    scores = scores + jnp.concatenate([bias] * HALF_HEADS, axis=1)
    raised = jnp.exp2(scores - jnp.max(scores, axis=0, keepdims=True))
    probs = (raised * (1.0 / jnp.sum(raised, axis=0, keepdims=True))).astype(bf16)
    return by_head(value, probs), probs


def attend_back(grad, query, key, value, probs):
    grad_apart = heads_apart(grad)
    grad_probs = dot_nt(value, grad_apart)
    wide = probs.astype(f32)
    inner = jnp.sum(grad_probs * wide, axis=0, keepdims=True)
    grad_scores = (wide * (grad_probs - inner)).astype(bf16)
    grad_value = dot(probs, grad_apart)
    grad_key = dot(grad_scores, heads_apart(query)) * factor
    grad_query = by_head(key, grad_scores) * factor
    return grad_query, grad_key, grad_value


def tap_of(taps, orient, major_step, minor_step):
    if orient == 0:
        return taps[3 * (major_step + 1) + minor_step + 1]
    return taps[3 * (minor_step + 1) + major_step + 1]


def tap_index(orient, major_step, minor_step):
    if orient == 0:
        return 3 * (major_step + 1) + minor_step + 1
    return 3 * (minor_step + 1) + major_step + 1


def minor_shifts(x):
    rows = x.shape[0]
    return {-1: pltpu.roll(x, 1, 0), 0: x, 1: pltpu.roll(x, rows - 1, 0)}


def major_shift(x, step):
    if step == 0:
        return x
    zeros = jnp.zeros((MINOR, x.shape[1]), x.dtype)
    if step == 1:
        return jnp.concatenate([x[MINOR:], zeros], axis=0)
    return jnp.concatenate([zeros, x[:-MINOR]], axis=0)


def stencil(value_shifts, taps, orient):
    out = None
    for major_step in (-1, 0, 1):
        line = None
        for minor_step in (-1, 0, 1):
            term = value_shifts[minor_step] * tap_of(taps, orient, major_step, minor_step)
            line = term if line is None else line + term
        line = major_shift(line, major_step)
        out = line if out is None else out + line
    return out + taps[9]


def stencil_back(grad_shifts, taps, orient):
    out = None
    for major_step in (-1, 0, 1):
        line = None
        for minor_step in (-1, 0, 1):
            term = grad_shifts[-minor_step] * tap_of(taps, orient, major_step, minor_step)
            line = term if line is None else line + term
        line = major_shift(line, -major_step)
        out = line if out is None else out + line
    return out


def stencil_tap_grads(grad, value_shifts, orient):
    sums = [None] * 9
    for major_step in (-1, 0, 1):
        for minor_step in (-1, 0, 1):
            shifted = value_shifts[minor_step]
            if major_step == 1:
                product = grad[:-MINOR] * shifted[MINOR:]
            elif major_step == -1:
                product = grad[MINOR:] * shifted[:-MINOR]
            else:
                product = grad * shifted
            sums[tap_index(orient, major_step, minor_step)] = column_sum(product)
    sums.append(column_sum(grad))
    return jnp.concatenate(sums, axis=0)


def assemble_attn(me, core, own, near, far, wqkv, wm, sm):
    half = ATTN_ROWS // 2
    for k in range(4):
        shard = lax.rem(me + 4 - k, 4)
        orient, part = lax.div(shard, 2), lax.rem(shard, 2)
        if k == 0:
            unit = own[...]
        else:
            first = jnp.where(core == 0, near[k - 1][...], far[k - 1][...])
            second = jnp.where(core == 0, far[k - 1][...], near[k - 1][...])
            unit = jnp.concatenate([first, second], axis=0)
        for p in range(3):
            at = pl.multiple_of(orient * 384 + p * 128 + part * 64, 64)
            wqkv[pl.ds(at, 64), :] = unit[p * 64 : (p + 1) * 64]
        wm[pl.ds(pl.multiple_of(shard * 64, 64), 64), :] = unit[192:256]
        vectors = unit[256:288].astype(f32)
        if k == 0:
            sm[...] = vectors
        else:
            sm[...] += vectors


def assemble_ff(me, core, own, near, far, we, wr):
    for k in range(4):
        shard = lax.rem(me + 4 - k, 4)
        if k == 0:
            first, second = own[:256], own[256:]
        else:
            first = jnp.where(core == 0, near[k - 1][...], far[k - 1][...])
            second = jnp.where(core == 0, far[k - 1][...], near[k - 1][...])
        we[shard] = first
        at = pl.multiple_of(shard * 64, 64)
        for c in range(4):
            wr[pl.ds(at, 64), c * 256 : (c + 1) * 256] = second[c * 64 : (c + 1) * 64]


def attn_forward(x, hw, crop0, turn, wqkv, wm, sm, a_ref, qkv_ref, probs_ref, mixed_ref):
    normal, _ = norm(x)
    a = (normal * sm[GAIN : GAIN + 1] + sm[SHIFT : SHIFT + 1]).astype(bf16)
    a_ref[...] = a
    entry = sm[ENTRY : ENTRY + 2]
    taps_all = sm[TAPS : TAPS + 10]
    inside = minor_inside(TOK, 128)
    for i in range(CB):
        rows = slice(i * TOK, (i + 1) * TOK)
        height, width = hw[2 * (crop0 + i)], hw[2 * (crop0 + i) + 1]
        a_here = a[rows]
        mixed_halves = []
        for orient in range(2):
            lanes = slice(orient * 128, (orient + 1) * 128)
            source = a_here if orient == 0 else dot(turn, a_here).astype(bf16)
            packed = dot_nt(source, wqkv[orient * 384 : (orient + 1) * 384])
            query = (packed[:, :128] + entry[0:1, lanes]).astype(bf16)
            key = packed[:, 128:256].astype(bf16)
            value = jnp.where(inside, packed[:, 256:] + entry[1:2, lanes], 0.0).astype(bf16)
            base = orient * 384
            qkv_ref[rows, base : base + 128] = query
            qkv_ref[rows, base + 128 : base + 256] = key
            qkv_ref[rows, base + 256 : base + 384] = value
            shifts = minor_shifts(value.astype(f32))
            taps = [taps_all[t : t + 1, lanes] for t in range(10)]
            major_end, minor_end = (height, width) if orient == 0 else (width, height)
            outs = []
            for window in range(2):
                win = slice(window * WIN, (window + 1) * WIN)
                bias = key_bias(major_end, minor_end, window)
                out, probs = attend(query[win], key[win], value[win], bias)
                probs_ref[i, 2 * orient + window] = probs
                out = out + stencil({s: v[win] for s, v in shifts.items()}, taps, orient)
                outs.append(out.astype(bf16))
            half = jnp.concatenate(outs, axis=0)
            if orient == 1:
                half = dot(turn, half).astype(bf16)
            mixed_halves.append(half)
        mixed_ref[rows, :] = jnp.concatenate(mixed_halves, axis=1)
    return x + (dot_nt(mixed_ref[...], wm[...]) + sm[BRANCH : BRANCH + 1])


def ff_forward(middle, we, wr, sm, a2_ref, g_ref, slope_ref):
    normal, _ = norm(middle)
    a2 = (normal * sm[GAIN + 1 : GAIN + 2] + sm[SHIFT + 1 : SHIFT + 2]).astype(bf16)
    a2_ref[...] = a2
    for s in range(4):
        u = dot(a2, we[s]) + sm[HIDDEN + s : HIDDEN + s + 1]
        phi = 0.5 + 0.5 * lax.erf(u * root_half)
        g_ref[:, s * 256 : (s + 1) * 256] = (u * phi).astype(bf16)
        slope_ref[:, s * 256 : (s + 1) * 256] = (
            phi + u * jnp.exp(-0.5 * u * u) * inverse_root_tau
        ).astype(bf16)
    return middle + (dot_nt(g_ref[...], wr[...]) + sm[BRANCH + 1 : BRANCH + 2])


def ff_backward(grad, middle, a2_ref, g_ref, slope_ref, we, wr, sm, acc_e, acc_r, vec):
    ey = grad.astype(bf16)
    vec[BRANCH + 1 : BRANCH + 2] += column_sum(grad)
    a2 = a2_ref[...]
    back = None
    for s in range(4):
        cols = slice(s * 256, (s + 1) * 256)
        acc_r[s] += dot_tn(ey, g_ref[:, cols])
        eu_wide = dot(ey, wr[:, cols]) * slope_ref[:, cols].astype(f32)
        vec[HIDDEN + s : HIDDEN + s + 1] += column_sum(eu_wide)
        eu = eu_wide.astype(bf16)
        acc_e[s] += dot_tn(a2, eu)
        term = dot_nt(eu, we[s])
        back = term if back is None else back + term
    normal, inverse = norm(middle)
    vec[GAIN + 1 : GAIN + 2] += column_sum(back * normal)
    vec[SHIFT + 1 : SHIFT + 2] += column_sum(back)
    return grad + norm_back(back, normal, inverse, sm[GAIN + 1 : GAIN + 2])


def attn_backward(grad, x, turn, a_ref, qkv_ref, probs_ref, mixed_ref, wqkv, wm, sm, e_ref, acc_q, acc_m, vec):
    eo = grad.astype(bf16)
    vec[BRANCH : BRANCH + 1] += column_sum(grad)
    acc_m[...] += dot_tn(eo, mixed_ref[...])
    em_all = dot(eo, wm[...]).astype(bf16)
    taps_all = sm[TAPS : TAPS + 10]
    inside = minor_inside(TOK, 128)
    for i in range(CB):
        rows = slice(i * TOK, (i + 1) * TOK)
        for orient in range(2):
            lanes = slice(orient * 128, (orient + 1) * 128)
            em = em_all[rows, lanes]
            if orient == 1:
                em = dot(turn, em).astype(bf16)
            base = orient * 384
            query = qkv_ref[rows, base : base + 128]
            key = qkv_ref[rows, base + 128 : base + 256]
            value = qkv_ref[rows, base + 256 : base + 384]
            taps = [taps_all[t : t + 1, lanes] for t in range(10)]
            em_wide = em.astype(f32)
            grad_shifts = minor_shifts(em_wide)
            value_shifts = minor_shifts(value.astype(f32))
            tap_grads = None
            got = [[], [], []]
            for window in range(2):
                win = slice(window * WIN, (window + 1) * WIN)
                dq, dk, dv = attend_back(em[win], query[win], key[win], value[win], probs_ref[i, 2 * orient + window])
                dv = dv + stencil_back({s: v[win] for s, v in grad_shifts.items()}, taps, orient)
                here = stencil_tap_grads(em_wide[win], {s: v[win] for s, v in value_shifts.items()}, orient)
                tap_grads = here if tap_grads is None else tap_grads + here
                got[0].append(dq)
                got[1].append(dk)
                got[2].append(dv)
            vec[TAPS : TAPS + 10, lanes] += tap_grads
            eq = jnp.concatenate(got[0], axis=0)
            ek = jnp.concatenate(got[1], axis=0)
            ev = jnp.where(inside, jnp.concatenate(got[2], axis=0), 0.0)
            vec[ENTRY : ENTRY + 1, lanes] += column_sum(eq)
            vec[ENTRY + 1 : ENTRY + 2, lanes] += column_sum(ev)
            e = jnp.concatenate([eq, ek, ev], axis=1).astype(bf16)
            if orient == 1:
                e = dot(turn, e).astype(bf16)
            e_ref[rows, base : base + 384] = e
    e = e_ref[...]
    acc_q[...] += dot_tn(e, a_ref[...])
    back = dot(e, wqkv[...])
    normal, inverse = norm(x)
    vec[GAIN : GAIN + 1] += column_sum(back * normal)
    vec[SHIFT : SHIFT + 1] += column_sum(back)
    return grad + norm_back(back, normal, inverse, sm[GAIN : GAIN + 1])


def write_ff_grads(out, acc_e, acc_r):
    for s in range(4):
        out[s, 0:256] = acc_e[s].astype(out.dtype)
        for c in range(4):
            out[s, 256 + 64 * c : 320 + 64 * c] = acc_r[c, 64 * s : 64 * (s + 1)].astype(out.dtype)


def write_attn_grads(out, acc_q, acc_m, vec):
    for s in range(4):
        for p in range(3):
            at = (s // 2) * 384 + p * 128 + (s % 2) * 64
            out[s, p * 64 : (p + 1) * 64] = acc_q[at : at + 64].astype(out.dtype)
        out[s, 192:256] = acc_m[64 * s : 64 * (s + 1)].astype(out.dtype)
        out[s, 256:288] = vec[...].astype(out.dtype)
        out[s, 288:320] = jnp.zeros((32, D), out.dtype)


def load_cells(ref, spread):
    spread[:, GRID:MINOR, :] = jnp.zeros((CB * GRID, MINOR - GRID, D), f32)
    spread[:, 0:GRID, :] = ref[...].reshape(CB * GRID, GRID, D).astype(f32)
    return spread[...].reshape(CB * TOK, D)


def store_cells(ref, x):
    cells = x.astype(ref.dtype).reshape(CB * GRID, MINOR, D)[:, 0:GRID, :]
    ref[...] = cells.reshape(CB, GRID, GRID, D)


def first_step(fn):
    pl.when(pl.program_id(0) == 0)(fn)


def last_step(fn):
    pl.when(pl.program_id(0) == pl.num_programs(0) - 1)(fn)


def attn_fwd_kernel(place, x, *refs):
    own, near, far = refs[0], refs[1:4], refs[4:7]
    mid, a, qkv, probs, mixed, wqkv, wm, sm, spread, turn = refs[7:]

    @first_step
    def _():
        assemble_attn(place[0], place[1], own, near, far, wqkv, wm, sm)
        turn[...] = grid_transpose()

    state = load_cells(x, spread)
    mid[...] = attn_forward(state, place, pl.program_id(0) * CB + 1, turn[...], wqkv, wm, sm, a, qkv, probs, mixed)


def ff_fwd_kernel(place, middle, sm, *refs):
    own, near, far = refs[0], refs[1:4], refs[4:7]
    out, a2, g, slope, we, wr = refs[7:]

    @first_step
    def _():
        assemble_ff(place[0], place[1], own, near, far, we, wr)

    out[...] = ff_forward(middle[...], we, wr, sm, a2, g, slope)


def top_kernel(place, x, cotangent, *refs):
    attn_in, ff_in = refs[0:7], refs[7:14]
    (output, grad_out, grads_a, grads_f) = refs[14:18]
    (wqkv, wm, sm, we, wr, turn, spread, middle, a, qkv, probs, mixed, a2, g, slope, e,
     acc_e, acc_r, acc_q, acc_m, vec) = refs[18:]

    @first_step
    def _():
        assemble_attn(place[0], place[1], attn_in[0], attn_in[1:4], attn_in[4:7], wqkv, wm, sm)
        assemble_ff(place[0], place[1], ff_in[0], ff_in[1:4], ff_in[4:7], we, wr)
        turn[...] = grid_transpose()
        for ref in (acc_e, acc_r, acc_q, acc_m, vec):
            ref[...] = jnp.zeros_like(ref)

    flip = turn[...]
    middle[...] = attn_forward(x[...], place, pl.program_id(0) * CB + 1, flip, wqkv, wm, sm, a, qkv, probs, mixed)
    store_cells(output, ff_forward(middle[...], we, wr, sm, a2, g, slope))
    grad = load_cells(cotangent, spread)
    grad_mid = ff_backward(grad, middle[...], a2, g, slope, we, wr, sm, acc_e, acc_r, vec)
    grad_out[...] = attn_backward(grad_mid, x[...], flip, a, qkv, probs, mixed, wqkv, wm, sm, e, acc_q, acc_m, vec)

    @last_step
    def _():
        write_ff_grads(grads_f, acc_e, acc_r)
        write_attn_grads(grads_a, acc_q, acc_m, vec)


def ff_bwd_kernel(grad, middle, a2, g, slope, we, wr, sm, grad_mid, grads_f, vec, acc_e, acc_r):
    @first_step
    def _():
        for ref in (acc_e, acc_r, vec):
            ref[...] = jnp.zeros_like(ref)

    grad_mid[...] = ff_backward(grad[...], middle[...], a2, g, slope, we, wr, sm, acc_e, acc_r, vec)

    @last_step
    def _():
        write_ff_grads(grads_f, acc_e, acc_r)


def attn_bwd_kernel(grad, x, a, qkv, probs, mixed, wqkv, wm, sm, vec_in, patch_grad, grads_a, spread, turn, e, acc_q, acc_m, vec):
    @first_step
    def _():
        for ref in (acc_q, acc_m):
            ref[...] = jnp.zeros_like(ref)
        vec[...] = vec_in[...]
        turn[...] = grid_transpose()

    state = load_cells(x, spread)
    store_cells(
        patch_grad,
        attn_backward(grad[...], state, turn[...], a, qkv, probs, mixed, wqkv, wm, sm, e, acc_q, acc_m, vec),
    )

    @last_step
    def _():
        write_attn_grads(grads_a, acc_q, acc_m, vec)


def whole(shape):
    return pl.BlockSpec(shape, lambda i, *_: (0,) * len(shape))


def rows_of(lanes):
    return pl.BlockSpec((CB * TOK, lanes), lambda i, *_: (i, 0))


def cells():
    return pl.BlockSpec((CB, GRID, GRID, D), lambda i, *_: (i, 0, 0, 0))


def probs_spec():
    return pl.BlockSpec((CB, 4, WIN, 512), lambda i, *_: (i, 0, 0, 0))


def unit_specs(rows):
    return [whole((rows, D))] + [whole((rows // 2, D))] * 6


def shape(dims, dtype=bf16):
    return jax.ShapeDtypeStruct(dims, dtype)


params = dict(
    compiler_params=pltpu.CompilerParams(
        vmem_limit_bytes=56 * 1024 * 1024, dimension_semantics=("arbitrary",)
    )
)


def attn_fwd_call(place, patches, unit):
    crops = patches.shape[0]
    n = crops * TOK
    return pl.pallas_call(
        attn_fwd_kernel,
        grid_spec=pltpu.PrefetchScalarGridSpec(
            num_scalar_prefetch=1,
            grid=(crops // CB,),
            in_specs=[cells()] + unit_specs(ATTN_ROWS),
            out_specs=[rows_of(D), rows_of(D), rows_of(768), probs_spec(), rows_of(D), whole((768, D)), whole((D, D)), whole((32, D))],
            scratch_shapes=[pltpu.VMEM((CB * GRID, MINOR, D), f32), pltpu.VMEM((TOK, TOK), bf16)],
        ),
        out_shape=[shape((n, D), f32), shape((n, D)), shape((n, 768)), shape((crops, 4, WIN, 512)), shape((n, D)), shape((768, D)), shape((D, D)), shape((32, D), f32)],
        name="attn_fwd",
        **params,
    )(place, patches, *unit)


def ff_fwd_call(place, middle, sm, unit):
    n = middle.shape[0]
    return pl.pallas_call(
        ff_fwd_kernel,
        grid_spec=pltpu.PrefetchScalarGridSpec(
            num_scalar_prefetch=1,
            grid=(n // (CB * TOK),),
            in_specs=[rows_of(D), whole((32, D))] + unit_specs(FF_ROWS),
            out_specs=[rows_of(D), rows_of(D), rows_of(FF), rows_of(FF), whole((4, D, D)), whole((D, FF))],
        ),
        out_shape=[shape((n, D), f32), shape((n, D)), shape((n, FF)), shape((n, FF)), shape((4, D, D)), shape((D, FF))],
        name="ff_fwd",
        **params,
    )(place, middle, sm, *unit)


def top_call(place, x, cotangent, attn_unit, ff_unit):
    n = x.shape[0]
    crops = n // TOK
    r = CB * TOK
    v = pltpu.VMEM
    return pl.pallas_call(
        top_kernel,
        grid_spec=pltpu.PrefetchScalarGridSpec(
            num_scalar_prefetch=1,
            grid=(crops // CB,),
            in_specs=[rows_of(D), cells()] + unit_specs(ATTN_ROWS) + unit_specs(FF_ROWS),
            out_specs=[cells(), rows_of(D), whole((4, GRAD_ATTN_ROWS, D)), whole((4, FF_ROWS, D))],
            scratch_shapes=[
                v((768, D), bf16), v((D, D), bf16), v((32, D), f32), v((4, D, D), bf16), v((D, FF), bf16),
                v((TOK, TOK), bf16), v((CB * GRID, MINOR, D), f32), v((r, D), f32), v((r, D), bf16), v((r, 768), bf16),
                v((CB, 4, WIN, 512), bf16), v((r, D), bf16), v((r, D), bf16), v((r, FF), bf16), v((r, FF), bf16), v((r, 768), bf16),
                v((4, D, D), f32), v((4, D, D), f32), v((768, D), f32), v((D, D), f32), v((32, D), f32),
            ],
        ),
        out_shape=[shape((crops, GRID, GRID, D)), shape((n, D), f32), shape((4, GRAD_ATTN_ROWS, D)), shape((4, FF_ROWS, D))],
        name="top_block",
        **params,
    )(place, x, cotangent, *attn_unit, *ff_unit)


def ff_bwd_call(grad, middle, a2, g, slope, we, wr, sm):
    n = grad.shape[0]
    return pl.pallas_call(
        ff_bwd_kernel,
        grid=(n // (CB * TOK),),
        in_specs=[rows_of(D), rows_of(D), rows_of(D), rows_of(FF), rows_of(FF), whole((4, D, D)), whole((D, FF)), whole((32, D))],
        out_specs=[rows_of(D), whole((4, FF_ROWS, D)), whole((32, D))],
        scratch_shapes=[pltpu.VMEM((4, D, D), f32), pltpu.VMEM((4, D, D), f32)],
        out_shape=[shape((n, D), f32), shape((4, FF_ROWS, D)), shape((32, D), f32)],
        name="ff_bwd",
        **params,
    )(grad, middle, a2, g, slope, we, wr, sm)


def attn_bwd_call(grad, patches, a, qkv, probs, mixed, wqkv, wm, sm, vec):
    crops = patches.shape[0]
    v = pltpu.VMEM
    return pl.pallas_call(
        attn_bwd_kernel,
        grid=(crops // CB,),
        in_specs=[rows_of(D), cells(), rows_of(D), rows_of(768), probs_spec(), rows_of(D), whole((768, D)), whole((D, D)), whole((32, D)), whole((32, D))],
        out_specs=[cells(), whole((4, GRAD_ATTN_ROWS, D))],
        scratch_shapes=[v((CB * GRID, MINOR, D), f32), v((TOK, TOK), bf16), v((CB * TOK, 768), bf16), v((768, D), f32), v((D, D), f32), v((32, D), f32)],
        out_shape=[shape(patches.shape), shape((4, GRAD_ATTN_ROWS, D))],
        name="attn_bwd",
        **params,
    )(grad, patches, a, qkv, probs, mixed, wqkv, wm, sm, vec)


def compute(place, patches, cotangent, attn_units, ff_units):
    mid, a, qkv, probs, mixed, wqkv, wm, sm = attn_fwd_call(place, patches, attn_units[0])
    state, a2, g, slope, we, wr = ff_fwd_call(place, mid, sm, ff_units[0])
    output, grad, grads_a1, grads_f1 = top_call(place, state, cotangent, attn_units[1], ff_units[1])
    grad_mid, grads_f0, vec = ff_bwd_call(grad, mid, a2, g, slope, we, wr, sm)
    patch_grad, grads_a0 = attn_bwd_call(grad_mid, patches, a, qkv, probs, mixed, wqkv, wm, sm, vec)
    return output, patch_grad, grads_a0, grads_f0, grads_a1, grads_f1


def pack_units(norm_gain, norm_shift, qkv_weight, entry_bias, stencil_taps, mixer_weight, branch_bias, expand_weight, hidden_bias, reduce_weight):
    layers = qkv_weight.shape[0]
    me = lax.axis_index("mp")
    qkv = jnp.transpose(qkv_weight, (0, 2, 3, 1)).reshape(layers, 192, D)
    mixer = jnp.transpose(mixer_weight, (0, 2, 1))
    vectors = jnp.concatenate([norm_gain, norm_shift, entry_bias, stencil_taps, branch_bias], axis=1)
    lane_shard = lax.broadcasted_iota(jnp.int32, (1, 1, D), 2) // 64
    vectors = jnp.where(lane_shard == me, jnp.tile(vectors, (1, 1, 4)), jnp.zeros((), bf16))
    row = lax.broadcasted_iota(jnp.int32, (1, 14, 1), 1)
    hidden = jnp.where(row == me, hidden_bias[:, None, :], jnp.zeros((), bf16))
    attn = jnp.concatenate([qkv, mixer, vectors, hidden], axis=1)
    reduce = jnp.transpose(reduce_weight, (0, 2, 1)).reshape(layers, 64, 4, D)
    reduce = jnp.transpose(reduce, (0, 2, 1, 3)).reshape(layers, D, D)
    ff = jnp.concatenate([expand_weight, reduce], axis=1)
    return [attn[i] for i in range(layers)], [ff[i] for i in range(layers)]


def turn_mp(x, k):
    n = lax.axis_size("mp")
    return lax.ppermute(x, "mp", [(i, (i + k) % n) for i in range(n)])


def swap_dp(x, bit):
    n = lax.axis_size("dp")
    return lax.ppermute(x, "dp", [(i, i ^ bit) for i in range(n)])


def gather_unit(unit, core):
    half = unit.shape[0] // 2
    mine = lax.dynamic_slice_in_dim(unit, core * half, half, 0)
    near = [turn_mp(mine, k) for k in (1, 2, 3)]
    far = [swap_dp(x, 1) for x in near]
    return [unit] + near + far


def sum_grads(grads, dtype=bf16):
    dp, me_dp, me = lax.axis_size("dp"), lax.axis_index("dp"), lax.axis_index("mp")
    rows = grads.shape[1]
    held = grads.reshape(4, dp, rows // dp, D)
    bit = 1
    held = grads.reshape(4, dp, rows // dp, D)
    while bit < dp:
        pairs = held.reshape(4, held.shape[1] // 2, 2, rows // dp, D)
        mine_at = (me_dp // bit) % 2
        keep = lax.dynamic_index_in_dim(pairs, mine_at, 2, keepdims=False)
        give = lax.dynamic_index_in_dim(pairs, 1 - mine_at, 2, keepdims=False)
        held = (keep.astype(f32) + swap_dp(give, bit).astype(f32)).astype(dtype)
        bit *= 2
    piece = held[:, 0]
    total = lax.dynamic_index_in_dim(piece, me, 0, keepdims=False).astype(f32)
    for k in (1, 2, 3):
        give = lax.dynamic_index_in_dim(piece, (me + k) % 4, 0, keepdims=False)
        total = total + turn_mp(give, k).astype(f32)
    return lax.all_gather(total, "dp", axis=0, tiled=True)


def piece_order(dp):
    return list(range(dp))


def unpack(attn, ff, me):
    layers = attn.shape[0]
    packed = jnp.transpose(attn[:, :192].reshape(layers, 3, 64, D), (0, 3, 1, 2))
    mixer = jnp.transpose(attn[:, 192:256], (0, 2, 1))
    vec = lax.dynamic_slice_in_dim(attn[:, 256:274], me * 64, 64, 2)
    hidden = lax.dynamic_index_in_dim(attn[:, 256 + HIDDEN : 256 + HIDDEN + 4], me, 1, keepdims=False)
    expand = ff[:, :256]
    reduce = jnp.transpose(ff[:, 256:].reshape(layers, 4, 64, D), (0, 1, 3, 2)).reshape(layers, FF, 64)
    return (
        vec[:, GAIN : GAIN + 2], vec[:, SHIFT : SHIFT + 2], packed, vec[:, ENTRY : ENTRY + 2], vec[:, TAPS : TAPS + 10],
        mixer, vec[:, BRANCH : BRANCH + 2], expand, hidden, reduce,
    )


def body(patches, validity, *rest):
    weights, cotangent = rest[:-1], rest[-1]
    me, core = lax.axis_index("mp"), lax.axis_index("dp") % 2
    heights = jnp.sum(validity[:, :, 0], axis=1)
    widths = jnp.sum(validity[:, 0, :], axis=1)
    place = jnp.concatenate([jnp.stack([me, core]), jnp.stack([heights, widths], axis=1).reshape(-1)]).astype(jnp.int32)
    attn, ff = pack_units(*weights)
    attn_units = [gather_unit(x, core) for x in attn]
    ff_units = [gather_unit(x, core) for x in ff]
    output, patch_grad, grads_a0, grads_f0, grads_a1, grads_f1 = compute(place, patches, cotangent, attn_units, ff_units)
    attn_sums = jnp.stack([sum_grads(grads_a0), sum_grads(grads_a1)])
    ff_sums = jnp.stack([sum_grads(grads_f0), sum_grads(grads_f1)])
    return (output, patch_grad) + unpack(attn_sums, ff_sums, me)


def solution(mesh):
    crops = P(("dp", "mp"), None, None, None)
    lanes = P(None, None, "mp")
    deep = P(None, None, None, "mp")
    return jax.shard_map(
        body,
        mesh=mesh,
        in_specs=(crops, P(("dp", "mp"), None, None), lanes, lanes, deep, lanes, lanes, lanes, lanes, lanes, P(None, "mp"), lanes, crops),
        out_specs=(crops, crops, lanes, lanes, deep, lanes, lanes, lanes, lanes, lanes, P(None, "mp"), lanes),
        check_vma=False,
    )
```

time: 955 us -> 253 us (0.26); the launches traced: 944 us -> 252 us
  local copies, waits for them, and re-layouts: 328 us -> 19.1 us
  blocking collectives: 318 us -> 37.3 us
  matrix products: 128 us -> 0 us
  Pallas kernels: 0 us -> 107 us
  other arithmetic: 81.6 us -> 7.9 us
  starting transfers between devices: 0.04 us -> 60.5 us
  waiting for transfers between devices: 71.2 us -> 19.5 us
  between operations: 17 us -> 1.39 us
    all_gather x20 -> x4, blocking collectives: 278 us -> 37.3 us  [sum_grads(): return lax.all_gather(total, 'dp', axis=0, tiled=True)]
    reshape x52 -> x3, local copies, waits for them, and re-layouts: 153 us -> 1.9 us  [the longest x1 0.97 us: pack_units(): reduce = jnp.transpose(reduce_weight, (0, 2, 1)).reshape(layers, 64, 4, D)]
    dot_general x44 -> x0, matrix products: 109 us -> none  [the longest x4 16.9 us: attend_back(): jnp.einsum('cwhqk,cwqhd->cwkhd', probs.astype(jnp.bfloat16), grad_window,...]
    pallas_call x0 -> x5, Pallas kernels: none -> 107 us  [the longest x1 46.5 us: top_call(): pl.pallas_call(top_kernel, grid_spec=pltpu.PrefetchScalarGridSpec(num_sca...]
    psum x1 -> x0, waiting for transfers between devices: 71.2 us -> none  [body(): lax.psum((stacked[0], stacked[1], stacked[2], stacked[3], stacked[4], sta...]
    ppermute x0 -> x48, starting transfers between devices: none -> 60.5 us  [the longest x24 46 us: turn_mp(): return lax.ppermute(x, 'mp', [(i, (i + k) % n) for i in range(n)])]
    slice x35 -> x3, local copies, waits for them, and re-layouts: 60.6 us -> 1.35 us  [the longest x1 0.75 us: pack_units(): return ([attn[i] for i in range(layers)], [ff[i] for i in range(layers)])]
    reduce_sum x16 -> x2, other arithmetic: 43.9 us -> 0.24 us  [the longest x1 0.13 us: body(): heights = jnp.sum(validity[:, :, 0], axis=1)]
  transfers between devices with their start and end apart: 1 -> 48, of which waited for: 1 -> 6; matrix products, arithmetic and copies ran while one was open for 5% -> 7% of each run, Pallas kernels for 0% -> 24%
where the time goes in v1:
time: 253 us; the launch traced here: 252 us
  Pallas kernels  107 us (42%)
  starting transfers between devices  60.5 us (24%)
  blocking collectives  37.3 us (15%)
  waiting for transfers between devices  19.5 us (8%)
  local copies, waits for them, and re-layouts  19.1 us (8%)
  other arithmetic  7.9 us (3%)
    pallas_call x1, Pallas kernels, top_call(): pl.pallas_call(top_kernel, grid_spec=pltpu.PrefetchScalarGridSpec(num_sca...  46.5 us
    ppermute x24, starting transfers between devices, turn_mp(): return lax.ppermute(x, 'mp', [(i, (i + k) % n) for i in range(n)])  46 us
    all_gather x4, blocking collectives, sum_grads(): return lax.all_gather(total, 'dp', axis=0, tiled=True)  37.3 us
    pallas_call x1, Pallas kernels, attn_bwd_call(): pl.pallas_call(attn_bwd_kernel, grid=(crops // CB,), in_specs=[rows_of(D)...  20.1 us
    pallas_call x1, Pallas kernels, attn_fwd_call(): pl.pallas_call(attn_fwd_kernel, grid_spec=pltpu.PrefetchScalarGridSpec(nu...  19.3 us
    ppermute x24, starting transfers between devices, swap_dp(): return lax.ppermute(x, 'dp', [(i, i ^ bit) for i in range(n)])  14.4 us
    unnamed x76, local copies, waits for them, and re-layouts  11.4 us
    pallas_call x1, Pallas kernels, ff_bwd_call(): pl.pallas_call(ff_bwd_kernel, grid=(n // (CB * TOK),), in_specs=[rows_of(...  11.1 us
  transfers between devices with their start and end apart: 48, of which 6 were waited for; matrix products, arithmetic and copies ran while one was open for 7% of the time, Pallas kernels for 24%

profile of v1, /device:TPU:0, one launch (start us, length us, event | category | flops | bytes accessed | tf_op | source)
XLA Modules:
  0.0 252.4 jit_solution(13246200555290547825)
XLA Ops:
  6.9 3.1 %collective-permute-start = (bf16[144,256]{1,0:T(8,128)(2,1)S(1)}, bf16[144,256]{1,0:T(8,128)(2,1)S(1)}, u32[]{:S(2)}, u32[]{:S(2)}) collective-permute-start(bf16[144,256]{1,0:T(8,128)(2,1)S(1)} %dynamic-slice_bitcast_fusion.10), channel_id=1, source_target_pairs={{0,1},{1,2},{2,3},{3,0},{4,5},{5,6},{6,7},{7,4},{8,9},{9,10},{10,1... | collective-permute-start | bytes 221192 | tf_op jit(solution)/shard_map/ppermute | solution.py:625
  10.0 2.6 %collective-permute-start.1 = (bf16[144,256]{1,0:T(8,128)(2,1)S(1)}, bf16[144,256]{1,0:T(8,128)(2,1)S(1)}, u32[]{:S(2)}, u32[]{:S(2)}) collective-permute-start(bf16[144,256]{1,0:T(8,128)(2,1)S(1)} %dynamic-slice_bitcast_fusion.10), channel_id=1, source_target_pairs={{0,2},{1,3},{2,0},{3,1},{4,6},{5,7},{6,4},{7,5},{8,10},{9,11},{10,... | collective-permute-start | bytes 221192 | tf_op jit(solution)/shard_map/ppermute | solution.py:625
  15.9 1.7 maximum_bitcast_fusion
  17.7 2.7 %collective-permute-start.7 = (bf16[256,256]{1,0:T(8,128)(2,1)S(1)}, bf16[256,256]{1,0:T(8,128)(2,1)S(1)}, u32[]{:S(2)}, u32[]{:S(2)}) collective-permute-start(bf16[256,256]{1,0:T(8,128)(2,1)S(1)} %dynamic-slice_bitcast_fusion.8), channel_id=1, source_target_pairs={{0,2},{1,3},{2,0},{3,1},{4,6},{5,7},{6,4},{7,5},{8,10},{9,11},{10,... | collective-permute-start | bytes 393224 | tf_op jit(solution)/shard_map/ppermute | solution.py:625
  20.6 4.2 %collective-permute-start.8 = (bf16[256,256]{1,0:T(8,128)(2,1)S(1)}, bf16[256,256]{1,0:T(8,128)(2,1)S(1)}, u32[]{:S(2)}, u32[]{:S(2)}) collective-permute-start(bf16[256,256]{1,0:T(8,128)(2,1)S(1)} %dynamic-slice_bitcast_fusion.8), channel_id=1, source_target_pairs={{0,3},{1,0},{2,1},{3,2},{4,7},{5,4},{6,5},{7,6},{8,11},{9,8},{10,9... | collective-permute-start | bytes 393224 | tf_op jit(solution)/shard_map/ppermute | solution.py:625
  26.2 5.0 %collective-permute-start.14 = (bf16[144,256]{1,0:T(8,128)(2,1)S(1)}, bf16[144,256]{1,0:T(8,128)(2,1)}, u32[]{:S(2)}, u32[]{:S(2)}) collective-permute-start(bf16[144,256]{1,0:T(8,128)(2,1)S(1)} %dynamic-slice_bitcast_fusion.9), channel_id=1, source_target_pairs={{0,3},{1,0},{2,1},{3,2},{4,7},{5,4},{6,5},{7,6},{8,11},{9,8},{10,9... | collective-permute-start | bytes 221192 | tf_op jit(solution)/shard_map/ppermute | solution.py:625
  31.2 5.5 %collective-permute-done.14.refs_3_ = bf16[144,256]{1,0:T(8,128)(2,1)} collective-permute-done((bf16[144,256]{1,0:T(8,128)(2,1)S(1)}, bf16[144,256]{1,0:T(8,128)(2,1)}, u32[]{:S(2)}, u32[]{:S(2)}) %collective-permute-start.14) | collective-permute-done | bytes 73760 | tf_op jit(solution)/shard_map/ppermute | solution.py:625
  36.7 2.3 collective-permute-start.19
  39.0 3.5 %collective-permute-start.20 = (bf16[256,256]{1,0:T(8,128)(2,1)S(1)}, bf16[256,256]{1,0:T(8,128)(2,1)S(1)}, u32[]{:S(2)}, u32[]{:S(2)}) collective-permute-start(bf16[256,256]{1,0:T(8,128)(2,1)S(1)} %fusion.12), channel_id=1, source_target_pairs={{0,3},{1,0},{2,1},{3,2},{4,7},{5,4},{6,5},{7,6},{8,11},{9,8},{10,9... | collective-permute-start | bytes 393224 | tf_op jit(solution)/shard_map/ppermute | solution.py:625
  43.2 3.1 %collective-permute-done.19.refs_9_ = bf16[256,256]{1,0:T(8,128)(2,1)S(1)} collective-permute-done((bf16[256,256]{1,0:T(8,128)(2,1)S(1)}, bf16[256,256]{1,0:T(8,128)(2,1)S(1)}, u32[]{:S(2)}, u32[]{:S(2)}) %collective-permute-start.19) | collective-permute-done | bytes 131104 | tf_op jit(solution)/shard_map/ppermute | solution.py:625
  52.4 19.3 %attn_fwd.1 = (f32[1792,256]{1,0:T(8,128)}, bf16[1792,256]{1,0:T(8,128)(2,1)}, bf16[1792,768]{1,0:T(8,128)(2,1)}, bf16[8,4,112,512]{3,2,1,0:T(8,128)(2,1)}, bf16...) custom-call(s32[18]{0:T(128)} %pad_add_fusion.1.place, ...), custom_call_target="tpu_custom_call" | custom-call | tf_op jit(solution)/shard_map/attn_fwd/pallas_call | solution.py:512
  71.8 9.8 %ff_fwd.1 = (f32[1792,256]{1,0:T(8,128)}, bf16[1792,256]{1,0:T(8,128)(2,1)}, bf16[1792,1024]{1,0:T(8,128)(2,1)}, bf16[1792,1024]{1,0:T(8,128)(2,1)}, bf16[4,256,...) custom-call(s32[18]{0:T(128)} %pad_add_fusion.1.place, f32[1792,256]{1,0:T(8,128)} %get-tuple-element.35.middle, ...), custom_call_target="tpu_custom_call" | custom-call | tf_op jit(solution)/shard_map/ff_fwd/pallas_call | solution.py:529
  82.4 46.5 %top_block.1 = (bf16[8,14,14,256]{3,2,1,0:T(8,128)(2,1)}, f32[1792,256]{1,0:T(8,128)}, bf16[4,320,256]{2,1,0:T(8,128)(2,1)}, bf16[4,512,256]{2,1,0:T(8,128)(2,1)}) custom-call(s32[18]{0:T(128)} %pad_add_fusion.1.place, f32[1792,256]{1,0:T(8,128)} %get-tuple-element.37.x, bf16[8,14,14,256]{3,2,1,0:T(8,128)(2,1)} %copy.47.cotangent, ...), custom_call_target="tpu_custom_call" | custom-call | tf_op jit(solution)/shard_map/top_block/pallas_call | solution.py:548
  130.1 11.1 %ff_bwd.1 = (f32[1792,256]{1,0:T(8,128)}, bf16[4,512,256]{2,1,0:T(8,128)(2,1)}, f32[32,256]{1,0:T(8,128)}) custom-call(f32[1792,256]{1,0:T(8,128)} %get-tuple-element.39.grad, f32[1792,256]{1,0:T(8,128)} %get-tuple-element.35.middle, bf16[1792,256]{1,0:T(8,128)(2,1)} %get-tuple-element.40.a2, bf16[1792,1024]{1,0:T(8,128)(2,1)} %get-tuple-element.41.g, ...), custom_call_target="tpu_custom_call" | custom-call | tf_op jit(solution)/shard_map/ff_bwd/pallas_call | solution.py:570
  143.0 20.1 %attn_bwd.1 = (bf16[8,14,14,256]{3,2,1,0:T(8,128)(2,1)}, bf16[4,320,256]{2,1,0:T(8,128)(2,1)}) custom-call(f32[1792,256]{1,0:T(8,128)} %get-tuple-element.45.grad, bf16[8,14,14,256]{3,2,1,0:T(8,128)(2,1)} %copy.45.x, bf16[1792,256]{1,0:T(8,128)(2,1)} %get-tuple-element.46.a, bf16[1792,768]{1,0:T(8,128)(2,1)} %get-tuple-element.47.qkv, ...), custom_call_target="tpu_custom_call" | custom-call | tf_op jit(solution)/shard_map/attn_bwd/pallas_call | solution.py:585
  164.6 2.5 copy.57
  168.6 1.9 collective-permute-start.31
  170.9 4.8 %collective-permute-done.31 = bf16[4,2,40,256]{3,2,1,0:T(8,128)(2,1)S(1)} collective-permute-done((bf16[4,2,40,256]{3,2,1,0:T(8,128)(2,1)S(1)}, bf16[4,2,40,256]{3,2,1,0:T(8,128)(2,1)S(1)}, u32[]{:S(2)}, u32[]{:S(2)}) %collective-permute-start.31) | collective-permute-done | bytes 163872 | tf_op jit(solution)/shard_map/ppermute | solution.py:630
  175.8 2.0 collective-permute-start.32
  178.6 1.8 collective-permute-start.26
  180.7 1.5 collective-permute-start.37
  183.1 2.3 collective-permute-start.33
  185.4 3.2 %collective-permute-start.34 = (bf16[40,256]{1,0:T(8,128)(2,1)S(1)}, bf16[40,256]{1,0:T(8,128)(2,1)S(1)}, u32[]{:S(2)}, u32[]{:S(2)}) collective-permute-start(bf16[40,256]{1,0:T(8,128)(2,1)S(1)} %get-tuple-element.98), channel_id=1, source_target_pairs={{0,2},{1,3},{2,0},{3,1},{4,6},{5,7},{6,4},{7,5},{8,10},{9,11},{10,... | collective-permute-start | bytes 61448 | tf_op jit(solution)/shard_map/ppermute | solution.py:625
  190.7 2.5 %collective-permute-start.28 = (bf16[40,256]{1,0:T(8,128)(2,1)S(1)}, bf16[40,256]{1,0:T(8,128)(2,1)S(1)}, u32[]{:S(2)}, u32[]{:S(2)}) collective-permute-start(bf16[40,256]{1,0:T(8,128)(2,1)S(1)} %get-tuple-element.101), channel_id=1, source_target_pairs={{0,2},{1,3},{2,0},{3,1},{4,6},{5,7},{6,4},{7,5},{8,10},{9,11},{10,... | collective-permute-start | bytes 61448 | tf_op jit(solution)/shard_map/ppermute | solution.py:625
  194.4 9.4 %all_gather.13 = f32[320,256]{1,0:T(8,128)S(1)} all-gather(f32[40,256]{1,0:T(8,128)S(1)} %fusion.20), channel_id=1, replica_groups=mesh['dp'=8,'mp'=4] {'dp'}, dimensions={0}, use_global_device_ids=true | all-gather | bytes 368640 | tf_op jit(solution)/shard_map/all_gather | solution.py:659
  203.9 9.1 %all_gather.12 = f32[320,256]{1,0:T(8,128)S(1)} all-gather(f32[40,256]{1,0:T(8,128)S(1)} %fusion.22), channel_id=1, replica_groups=mesh['dp'=8,'mp'=4] {'dp'}, dimensions={0}, use_global_device_ids=true | all-gather | bytes 368640 | tf_op jit(solution)/shard_map/all_gather | solution.py:659
  218.7 4.1 %collective-permute-done.38 = bf16[4,1,64,256]{3,2,1,0:T(8,128)(2,1)S(1)} collective-permute-done((bf16[4,1,64,256]{3,2,1,0:T(8,128)(2,1)S(1)}, bf16[4,1,64,256]{3,2,1,0:T(8,128)(2,1)S(1)}, u32[]{:S(2)}, u32[]{:S(2)}) %collective-permute-start.38) | collective-permute-done | bytes 131104 | tf_op jit(solution)/shard_map/ppermute | solution.py:630
  223.6 3.2 %collective-permute-start.41 = (bf16[64,256]{1,0:T(8,128)(2,1)S(1)}, bf16[64,256]{1,0:T(8,128)(2,1)S(1)}, u32[]{:S(2)}, u32[]{:S(2)}) collective-permute-start(bf16[64,256]{1,0:T(8,128)(2,1)S(1)} %get-tuple-element.94), channel_id=1, source_target_pairs={{0,3},{1,0},{2,1},{3,2},{4,7},{5,4},{6,5},{7,6},{8,11},{9,8},{10,9... | collective-permute-start | bytes 98312 | tf_op jit(solution)/shard_map/ppermute | solution.py:625
  227.5 1.5 collective-permute-start.46
  229.0 2.8 %collective-permute-start.47 = (bf16[64,256]{1,0:T(8,128)(2,1)S(1)}, bf16[64,256]{1,0:T(8,128)(2,1)S(1)}, u32[]{:S(2)}, u32[]{:S(2)}) collective-permute-start(bf16[64,256]{1,0:T(8,128)(2,1)S(1)} %get-tuple-element.91), channel_id=1, source_target_pairs={{0,3},{1,0},{2,1},{3,2},{4,7},{5,4},{6,5},{7,6},{8,11},{9,8},{10,9... | collective-permute-start | bytes 98312 | tf_op jit(solution)/shard_map/ppermute | solution.py:625
  231.9 9.2 %all_gather.14 = f32[512,256]{1,0:T(8,128)S(1)} all-gather(f32[64,256]{1,0:T(8,128)S(1)} %fusion.18), channel_id=1, replica_groups=mesh['dp'=8,'mp'=4] {'dp'}, dimensions={0}, use_global_device_ids=true | all-gather | bytes 589824 | tf_op jit(solution)/shard_map/all_gather | solution.py:659
  241.1 9.5 %all_gather.15 = f32[512,256]{1,0:T(8,128)S(1)} all-gather(f32[64,256]{1,0:T(8,128)S(1)} %fusion.16), channel_id=1, replica_groups=mesh['dp'=8,'mp'=4] {'dp'}, dimensions={0}, use_global_device_ids=true | all-gather | bytes 589824 | tf_op jit(solution)/shard_map/all_gather | solution.py:659
  (210 shorter events, 39.1 us)
Async XLA Ops:
  6.9 10.7 %collective-permute-start = (bf16[144,256]{1,0:T(8,128)(2,1)S(1)}, bf16[144,256]{1,0:T(8,128)(2,1)S(1)}, u32[]{:S(2)}, u32[]{:S(2)}) collective-permute-start(bf16[144,256]{1,0:T(8,128)(2,1)S(1)} %dynamic-slice_bitcast_fusion.10), channel_id=1, source_target_pairs={{0,1},{1,2},{2,3},{3,0},{4,5},{5,6},{6,7},{7,4},{8,9},{9,10},{10,1... | collective-permute-start | bytes 221192 | tf_op jit(solution)/shard_map/ppermute | solution.py:625
  10.0 10.6 %collective-permute-start.1 = (bf16[144,256]{1,0:T(8,128)(2,1)S(1)}, bf16[144,256]{1,0:T(8,128)(2,1)S(1)}, u32[]{:S(2)}, u32[]{:S(2)}) collective-permute-start(bf16[144,256]{1,0:T(8,128)(2,1)S(1)} %dynamic-slice_bitcast_fusion.10), channel_id=1, source_target_pairs={{0,2},{1,3},{2,0},{3,1},{4,6},{5,7},{6,4},{7,5},{8,10},{9,11},{10,... | collective-permute-start | bytes 221192 | tf_op jit(solution)/shard_map/ppermute | solution.py:625
  12.6 12.3 %collective-permute-start.2 = (bf16[144,256]{1,0:T(8,128)(2,1)S(1)}, bf16[144,256]{1,0:T(8,128)(2,1)S(1)}, u32[]{:S(2)}, u32[]{:S(2)}) collective-permute-start(bf16[144,256]{1,0:T(8,128)(2,1)S(1)} %dynamic-slice_bitcast_fusion.10), channel_id=1, source_target_pairs={{0,3},{1,0},{2,1},{3,2},{4,7},{5,4},{6,5},{7,6},{8,11},{9,8},{10,9... | collective-permute-start | bytes 221192 | tf_op jit(solution)/shard_map/ppermute | solution.py:625
  13.9 10.9 %collective-permute-start.12 = (bf16[144,256]{1,0:T(8,128)(2,1)S(1)}, bf16[144,256]{1,0:T(8,128)(2,1)S(1)}, u32[]{:S(2)}, u32[]{:S(2)}) collective-permute-start(bf16[144,256]{1,0:T(8,128)(2,1)S(1)} %dynamic-slice_bitcast_fusion.9), channel_id=1, source_target_pairs={{0,1},{1,2},{2,3},{3,0},{4,5},{5,6},{6,7},{7,4},{8,9},{9,10},{10,1... | collective-permute-start | bytes 221192 | tf_op jit(solution)/shard_map/ppermute | solution.py:625
  14.6 11.6 %collective-permute-start.13 = (bf16[144,256]{1,0:T(8,128)(2,1)S(1)}, bf16[144,256]{1,0:T(8,128)(2,1)S(1)}, u32[]{:S(2)}, u32[]{:S(2)}) collective-permute-start(bf16[144,256]{1,0:T(8,128)(2,1)S(1)} %dynamic-slice_bitcast_fusion.9), channel_id=1, source_target_pairs={{0,2},{1,3},{2,0},{3,1},{4,6},{5,7},{6,4},{7,5},{8,10},{9,11},{10,... | collective-permute-start | bytes 221192 | tf_op jit(solution)/shard_map/ppermute | solution.py:625
  17.7 21.3 %collective-permute-start.7 = (bf16[256,256]{1,0:T(8,128)(2,1)S(1)}, bf16[256,256]{1,0:T(8,128)(2,1)S(1)}, u32[]{:S(2)}, u32[]{:S(2)}) collective-permute-start(bf16[256,256]{1,0:T(8,128)(2,1)S(1)} %dynamic-slice_bitcast_fusion.8), channel_id=1, source_target_pairs={{0,2},{1,3},{2,0},{3,1},{4,6},{5,7},{6,4},{7,5},{8,10},{9,11},{10,... | collective-permute-start | bytes 393224 | tf_op jit(solution)/shard_map/ppermute | solution.py:625
  20.6 21.9 %collective-permute-start.8 = (bf16[256,256]{1,0:T(8,128)(2,1)S(1)}, bf16[256,256]{1,0:T(8,128)(2,1)S(1)}, u32[]{:S(2)}, u32[]{:S(2)}) collective-permute-start(bf16[256,256]{1,0:T(8,128)(2,1)S(1)} %dynamic-slice_bitcast_fusion.8), channel_id=1, source_target_pairs={{0,3},{1,0},{2,1},{3,2},{4,7},{5,4},{6,5},{7,6},{8,11},{9,8},{10,9... | collective-permute-start | bytes 393224 | tf_op jit(solution)/shard_map/ppermute | solution.py:625
  24.9 17.7 %collective-permute-start.6 = (bf16[256,256]{1,0:T(8,128)(2,1)S(1)}, bf16[256,256]{1,0:T(8,128)(2,1)S(1)}, u32[]{:S(2)}, u32[]{:S(2)}) collective-permute-start(bf16[256,256]{1,0:T(8,128)(2,1)S(1)} %dynamic-slice_bitcast_fusion.8), channel_id=1, source_target_pairs={{0,1},{1,2},{2,3},{3,0},{4,5},{5,6},{6,7},{7,4},{8,9},{9,10},{10,1... | collective-permute-start | bytes 393224 | tf_op jit(solution)/shard_map/ppermute | solution.py:625
  24.9 18.1 %collective-permute-start.18 = (bf16[256,256]{1,0:T(8,128)(2,1)S(1)}, bf16[256,256]{1,0:T(8,128)(2,1)S(1)}, u32[]{:S(2)}, u32[]{:S(2)}) collective-permute-start(bf16[256,256]{1,0:T(8,128)(2,1)S(1)} %fusion.12), channel_id=1, source_target_pairs={{0,1},{1,2},{2,3},{3,0},{4,5},{5,6},{6,7},{7,4},{8,9},{9,10},{10,1... | collective-permute-start | bytes 393224 | tf_op jit(solution)/shard_map/ppermute | solution.py:625
  26.2 10.5 %collective-permute-start.14 = (bf16[144,256]{1,0:T(8,128)(2,1)S(1)}, bf16[144,256]{1,0:T(8,128)(2,1)}, u32[]{:S(2)}, u32[]{:S(2)}) collective-permute-start(bf16[144,256]{1,0:T(8,128)(2,1)S(1)} %dynamic-slice_bitcast_fusion.9), channel_id=1, source_target_pairs={{0,3},{1,0},{2,1},{3,2},{4,7},{5,4},{6,5},{7,6},{8,11},{9,8},{10,9... | collective-permute-start | bytes 221192 | tf_op jit(solution)/shard_map/ppermute | solution.py:625
  36.7 9.6 %collective-permute-start.19 = (bf16[256,256]{1,0:T(8,128)(2,1)S(1)}, bf16[256,256]{1,0:T(8,128)(2,1)S(1)}, u32[]{:S(2)}, u32[]{:S(2)}) collective-permute-start(bf16[256,256]{1,0:T(8,128)(2,1)S(1)} %fusion.12), channel_id=1, source_target_pairs={{0,2},{1,3},{2,0},{3,1},{4,6},{5,7},{6,4},{7,5},{8,10},{9,11},{10,... | collective-permute-start | bytes 393224 | tf_op jit(solution)/shard_map/ppermute | solution.py:625
  47.6 34.1 %collective-permute-start.21 = (bf16[256,256]{1,0:T(8,128)(2,1)S(1)}, bf16[256,256]{1,0:T(8,128)(2,1)S(1)}, u32[]{:S(2)}, u32[]{:S(2)}) collective-permute-start(bf16[256,256]{1,0:T(8,128)(2,1)S(1)} %collective-permute-done.18.refs_8_), channel_id=1, source_target_pairs={{0,4},{4,0},{8,12},{12,8},{16,20},{20,16},{24,28},{28,24},{1,5},{5... | collective-permute-start | bytes 393224 | tf_op jit(solution)/shard_map/ppermute | solution.py:630
  48.2 33.5 %collective-permute-start.22 = (bf16[256,256]{1,0:T(8,128)(2,1)S(1)}, bf16[256,256]{1,0:T(8,128)(2,1)S(1)}, u32[]{:S(2)}, u32[]{:S(2)}) collective-permute-start(bf16[256,256]{1,0:T(8,128)(2,1)S(1)} %collective-permute-done.19.refs_9_), channel_id=1, source_target_pairs={{0,4},{4,0},{8,12},{12,8},{16,20},{20,16},{24,28},{28,24},{1,5},{5... | collective-permute-start | bytes 393224 | tf_op jit(solution)/shard_map/ppermute | solution.py:630
  48.4 33.3 %collective-permute-start.23 = (bf16[256,256]{1,0:T(8,128)(2,1)S(1)}, bf16[256,256]{1,0:T(8,128)(2,1)S(1)}, u32[]{:S(2)}, u32[]{:S(2)}) collective-permute-start(bf16[256,256]{1,0:T(8,128)(2,1)S(1)} %collective-permute-done.20.refs_10_), channel_id=1, source_target_pairs={{0,4},{4,0},{8,12},{12,8},{16,20},{20,16},{24,28},{28,24},{1,5},{5... | collective-permute-start | bytes 393224 | tf_op jit(solution)/shard_map/ppermute | solution.py:630
  51.3 30.3 %collective-permute-start.16 = (bf16[144,256]{1,0:T(8,128)(2,1)}, bf16[144,256]{1,0:T(8,128)(2,1)S(1)}, u32[]{:S(2)}, u32[]{:S(2)}) collective-permute-start(bf16[144,256]{1,0:T(8,128)(2,1)} %copy-done.28), channel_id=1, source_target_pairs={{0,4},{4,0},{8,12},{12,8},{16,20},{20,16},{24,28},{28,24},{1,5},{5... | collective-permute-start | bytes 221192 | tf_op jit(solution)/shard_map/ppermute | solution.py:630
  51.5 30.2 %collective-permute-start.17 = (bf16[144,256]{1,0:T(8,128)(2,1)}, bf16[144,256]{1,0:T(8,128)(2,1)S(1)}, u32[]{:S(2)}, u32[]{:S(2)}) collective-permute-start(bf16[144,256]{1,0:T(8,128)(2,1)} %collective-permute-done.14.refs_3_), channel_id=1, source_target_pairs={{0,4},{4,0},{8,12},{12,8},{16,20},{20,16},{24,28},{28,24},{1,5},{5... | collective-permute-start | bytes 221192 | tf_op jit(solution)/shard_map/ppermute | solution.py:630
  129.9 38.6 %collective-permute-start.30 = (bf16[4,4,40,256]{3,2,1,0:T(8,128)(2,1)S(1)}, bf16[4,4,40,256]{3,2,1,0:T(8,128)(2,1)S(1)}, u32[]{:S(2)}, u32[]{:S(2)}) collective-permute-start(bf16[4,4,40,256]{3,2,1,0:T(8,128)(2,1)S(1)} %dynamic-slice_bitcast_fusion.2), channel_id=1, source_target_pairs={{0,4},{4,0},{8,12},{12,8},{16,20},{20,16},{24,28},{28,24},{1,5},{5... | collective-permute-start | bytes 983048 | tf_op jit(solution)/shard_map/ppermute | solution.py:630
  142.3 38.2 %collective-permute-start.36 = (bf16[4,4,64,256]{3,2,1,0:T(8,128)(2,1)S(1)}, bf16[4,4,64,256]{3,2,1,0:T(8,128)(2,1)S(1)}, u32[]{:S(2)}, u32[]{:S(2)}) collective-permute-start(bf16[4,4,64,256]{3,2,1,0:T(8,128)(2,1)S(1)} %dynamic-slice_bitcast_fusion.1), channel_id=1, source_target_pairs={{0,4},{4,0},{8,12},{12,8},{16,20},{20,16},{24,28},{28,24},{1,5},{5... | collective-permute-start | bytes 1572872 | tf_op jit(solution)/shard_map/ppermute | solution.py:630
  142.8 39.5 %collective-permute-start.42 = (bf16[4,4,64,256]{3,2,1,0:T(8,128)(2,1)S(1)}, bf16[4,4,64,256]{3,2,1,0:T(8,128)(2,1)S(1)}, u32[]{:S(2)}, u32[]{:S(2)}) collective-permute-start(bf16[4,4,64,256]{3,2,1,0:T(8,128)(2,1)S(1)} %dynamic-slice_bitcast_fusion), channel_id=1, source_target_pairs={{0,4},{4,0},{8,12},{12,8},{16,20},{20,16},{24,28},{28,24},{1,5},{5... | collective-permute-start | bytes 1572872 | tf_op jit(solution)/shard_map/ppermute | solution.py:630
  170.7 7.9 %collective-permute-start.25 = (bf16[4,2,40,256]{3,2,1,0:T(8,128)(2,1)S(1)}, bf16[4,2,40,256]{3,2,1,0:T(8,128)(2,1)S(1)}, u32[]{:S(2)}, u32[]{:S(2)}) collective-permute-start(bf16[4,2,40,256]{3,2,1,0:T(8,128)(2,1)S(1)} %dynamic-slice_bitcast_fusion.7), channel_id=1, source_target_pairs={{0,8},{4,12},{8,0},{12,4},{16,24},{20,28},{24,16},{28,20},{1,9},{5... | collective-permute-start | bytes 491528 | tf_op jit(solution)/shard_map/ppermute | solution.py:630
  178.6 10.0 %collective-permute-start.26 = (bf16[4,1,40,256]{3,2,1,0:T(8,128)(2,1)S(1)}, bf16[4,1,40,256]{3,2,1,0:T(8,128)(2,1)S(1)}, u32[]{:S(2)}, u32[]{:S(2)}) collective-permute-start(bf16[4,1,40,256]{3,2,1,0:T(8,128)(2,1)S(1)} %constant_dynamic-slice_fusion.4), channel_id=1, source_target_pairs={{0,16},{4,20},{8,24},{12,28},{16,0},{20,4},{24,8},{28,12},{1,17},{... | collective-permute-start | bytes 245768 | tf_op jit(solution)/shard_map/ppermute | solution.py:630
  180.7 35.7 %collective-permute-start.37 = (bf16[4,2,64,256]{3,2,1,0:T(8,128)(2,1)S(1)}, bf16[4,2,64,256]{3,2,1,0:T(8,128)(2,1)S(1)}, u32[]{:S(2)}, u32[]{:S(2)}) collective-permute-start(bf16[4,2,64,256]{3,2,1,0:T(8,128)(2,1)S(1)} %dynamic-slice_bitcast_fusion.5), channel_id=1, source_target_pairs={{0,8},{4,12},{8,0},{12,4},{16,24},{20,28},{24,16},{28,20},{1,9},{5... | collective-permute-start | bytes 786440 | tf_op jit(solution)/shard_map/ppermute | solution.py:630
  182.4 34.9 %collective-permute-start.43 = (bf16[4,2,64,256]{3,2,1,0:T(8,128)(2,1)S(1)}, bf16[4,2,64,256]{3,2,1,0:T(8,128)(2,1)S(1)}, u32[]{:S(2)}, u32[]{:S(2)}) collective-permute-start(bf16[4,2,64,256]{3,2,1,0:T(8,128)(2,1)S(1)} %dynamic-slice_bitcast_fusion.4), channel_id=1, source_target_pairs={{0,8},{4,12},{8,0},{12,4},{16,24},{20,28},{24,16},{28,20},{1,9},{5... | collective-permute-start | bytes 786440 | tf_op jit(solution)/shard_map/ppermute | solution.py:630
  189.8 14.1 %collective-permute-start.27 = (bf16[40,256]{1,0:T(8,128)(2,1)S(1)}, bf16[40,256]{1,0:T(8,128)(2,1)S(1)}, u32[]{:S(2)}, u32[]{:S(2)}) collective-permute-start(bf16[40,256]{1,0:T(8,128)(2,1)S(1)} %get-tuple-element.99), channel_id=1, source_target_pairs={{0,1},{1,2},{2,3},{3,0},{4,5},{5,6},{6,7},{7,4},{8,9},{9,10},{10,1... | collective-permute-start | bytes 61448 | tf_op jit(solution)/shard_map/ppermute | solution.py:625
  190.7 13.1 %collective-permute-start.28 = (bf16[40,256]{1,0:T(8,128)(2,1)S(1)}, bf16[40,256]{1,0:T(8,128)(2,1)S(1)}, u32[]{:S(2)}, u32[]{:S(2)}) collective-permute-start(bf16[40,256]{1,0:T(8,128)(2,1)S(1)} %get-tuple-element.101), channel_id=1, source_target_pairs={{0,2},{1,3},{2,0},{3,1},{4,6},{5,7},{6,4},{7,5},{8,10},{9,11},{10,... | collective-permute-start | bytes 61448 | tf_op jit(solution)/shard_map/ppermute | solution.py:625
  193.3 10.6 %collective-permute-start.29 = (bf16[40,256]{1,0:T(8,128)(2,1)S(1)}, bf16[40,256]{1,0:T(8,128)(2,1)S(1)}, u32[]{:S(2)}, u32[]{:S(2)}) collective-permute-start(bf16[40,256]{1,0:T(8,128)(2,1)S(1)} %get-tuple-element.100), channel_id=1, source_target_pairs={{0,3},{1,0},{2,1},{3,2},{4,7},{5,4},{6,5},{7,6},{8,11},{9,8},{10,9... | collective-permute-start | bytes 61448 | tf_op jit(solution)/shard_map/ppermute | solution.py:625
  217.4 9.3 %collective-permute-start.44 = (bf16[4,1,64,256]{3,2,1,0:T(8,128)(2,1)S(1)}, bf16[4,1,64,256]{3,2,1,0:T(8,128)(2,1)S(1)}, u32[]{:S(2)}, u32[]{:S(2)}) collective-permute-start(bf16[4,1,64,256]{3,2,1,0:T(8,128)(2,1)S(1)} %constant_dynamic-slice_fusion.1), channel_id=1, source_target_pairs={{0,16},{4,20},{8,24},{12,28},{16,0},{20,4},{24,8},{28,12},{1,17},{... | collective-permute-start | bytes 393224 | tf_op jit(solution)/shard_map/ppermute | solution.py:630
  223.2 8.7 %collective-permute-start.40 = (bf16[64,256]{1,0:T(8,128)(2,1)S(1)}, bf16[64,256]{1,0:T(8,128)(2,1)S(1)}, u32[]{:S(2)}, u32[]{:S(2)}) collective-permute-start(bf16[64,256]{1,0:T(8,128)(2,1)S(1)} %get-tuple-element.95), channel_id=1, source_target_pairs={{0,2},{1,3},{2,0},{3,1},{4,6},{5,7},{6,4},{7,5},{8,10},{9,11},{10,... | collective-permute-start | bytes 98312 | tf_op jit(solution)/shard_map/ppermute | solution.py:625
  223.6 8.2 %collective-permute-start.41 = (bf16[64,256]{1,0:T(8,128)(2,1)S(1)}, bf16[64,256]{1,0:T(8,128)(2,1)S(1)}, u32[]{:S(2)}, u32[]{:S(2)}) collective-permute-start(bf16[64,256]{1,0:T(8,128)(2,1)S(1)} %get-tuple-element.94), channel_id=1, source_target_pairs={{0,3},{1,0},{2,1},{3,2},{4,7},{5,4},{6,5},{7,6},{8,11},{9,8},{10,9... | collective-permute-start | bytes 98312 | tf_op jit(solution)/shard_map/ppermute | solution.py:625
  226.8 14.2 %collective-permute-start.45 = (bf16[64,256]{1,0:T(8,128)(2,1)S(1)}, bf16[64,256]{1,0:T(8,128)(2,1)S(1)}, u32[]{:S(2)}, u32[]{:S(2)}) collective-permute-start(bf16[64,256]{1,0:T(8,128)(2,1)S(1)} %get-tuple-element.90), channel_id=1, source_target_pairs={{0,1},{1,2},{2,3},{3,0},{4,5},{5,6},{6,7},{7,4},{8,9},{9,10},{10,1... | collective-permute-start | bytes 98312 | tf_op jit(solution)/shard_map/ppermute | solution.py:625
  227.5 13.6 %collective-permute-start.46 = (bf16[64,256]{1,0:T(8,128)(2,1)S(1)}, bf16[64,256]{1,0:T(8,128)(2,1)S(1)}, u32[]{:S(2)}, u32[]{:S(2)}) collective-permute-start(bf16[64,256]{1,0:T(8,128)(2,1)S(1)} %get-tuple-element.92), channel_id=1, source_target_pairs={{0,2},{1,3},{2,0},{3,1},{4,6},{5,7},{6,4},{7,5},{8,10},{9,11},{10,... | collective-permute-start | bytes 98312 | tf_op jit(solution)/shard_map/ppermute | solution.py:625
  229.0 12.1 %collective-permute-start.47 = (bf16[64,256]{1,0:T(8,128)(2,1)S(1)}, bf16[64,256]{1,0:T(8,128)(2,1)S(1)}, u32[]{:S(2)}, u32[]{:S(2)}) collective-permute-start(bf16[64,256]{1,0:T(8,128)(2,1)S(1)} %get-tuple-element.91), channel_id=1, source_target_pairs={{0,3},{1,0},{2,1},{3,2},{4,7},{5,4},{6,5},{7,6},{8,11},{9,8},{10,9... | collective-permute-start | bytes 98312 | tf_op jit(solution)/shard_map/ppermute | solution.py:625
  (49 other events, 725.9 us)
